TPU v7x, 128 devices: a whole 4x4x4 slice. The times are simulated.
128 devices in a mesh: ctx: 16 (over z, x_lo, core), tp: 8 (over x_hi, y).
Axes of the slice: x: 4 (x_hi: 2, x_lo: 2; x = x_hi * 2 + x_lo), y: 4, z: 4, core: 2. Of those that a mesh axis runs over, the one named last changes fastest.
Arguments:
- prefill_query: bfloat16 [4096, 12288], P('ctx', 'tp'), may hold values from -400 to 400
- span_latent: bfloat16 [4096, 576], P('ctx'), may hold values from -8 to 8
- prompt_lengths: int32 [8], replicated, may hold values from 1 to 2560, 4096 in all
- key_weight: bfloat16 [512, 8192], P(None, 'tp'), may hold values from -0.25 to 0.25
- value_weight: bfloat16 [512, 8192], P(None, 'tp'), may hold values from -0.25 to 0.25
- placement: int32 [8], replicated, may hold values from 0 to 255, as said below
- resident_cache: bfloat16 [256, 256, 576], P('ctx'), may hold values from -6 to 6
- resident_lengths: int32 [256], P('ctx'), may hold values from 1 to 256, 32768 in all
- decode_query: bfloat16 [256, 2, 12288], P('ctx', None, 'tp'), may hold values from -400 to 400
- decode_latent: bfloat16 [256, 2, 576], P('ctx'), may hold values from -8 to 8
- out_weight: bfloat16 [8192, 7168], P('tp'), may hold values from -0.0625 to 0.0625
Outputs:
- prefill_out: bfloat16 [4096, 8192], P('ctx', 'tp')
- decode_out: bfloat16 [256, 2, 7168], P(('ctx', 'tp'))
Inputs may be any that keep to these rules, and one draw needn't show every extreme that they name: `placement`: 8 distinct decode rows, one for each request of the span; row r belongs to decode group r // 16; exactly one group takes 2 requests and every other group at most one; row 0 and row 255 always take a request.
All inputs are finite; a program needn't handle non-finite values. No bound on the sum of `resident_lengths` on one device may be relied on, other than what follows from the above.
Results may differ from a plain program's by a relative error of at most 0.019.
Values may be sent and summed in bfloat16 or wider, within the bound.
A program may use at most 192 MiB of HBM per device.

v0:
```python
import math

import jax
import jax.numpy as jnp
from jax import lax
from jax.sharding import PartitionSpec as P

NOPE = 128
VHEAD = 128
NEW_DEV = 2


def product(form, left, right):
    return jnp.einsum(form, left, right, preferred_element_type=jnp.float32)


def segment_ids(positions, request_ends):
    return jnp.sum((positions[:, None] >= request_ends[None, :]).astype(jnp.int32), axis=1)


def attend_block(
    carried,
    query_plain,
    query_rope,
    key_plain,
    key_rope,
    value_rows,
    query_pos,
    query_seg,
    key_pos,
    key_seg,
    score_scale,
):
    running_max, weight_sum, accumulated = carried
    scores = (
        product("qhn,khn->qhk", query_plain, key_plain)
        + product("qhe,ke->qhk", query_rope, key_rope)
    ) * score_scale
    visible = ((query_seg[:, None] == key_seg[None, :]) & (key_pos[None, :] <= query_pos[:, None]))[
        :, None, :
    ]
    block_max = jnp.max(jnp.where(visible, scores, -jnp.inf), axis=2)
    new_max = jnp.maximum(running_max, block_max)
    weights = jnp.where(visible, jnp.exp(scores - new_max[:, :, None]), 0.0)
    weight_sum = jnp.sum(weights, axis=2)
    accumulated = product("qhk,khv->qhv", weights.astype(jnp.bfloat16), value_rows)
    return (new_max, weight_sum, accumulated)


def land_piece(landed, key_piece, first_key, slot_start, slot_length):
    piece_rows = key_piece.shape[0]
    slot_count = landed.shape[0]
    longest = landed.shape[1]
    window = min(piece_rows, longest)
    zeros_pad = jnp.zeros((window, key_piece.shape[1]), key_piece.dtype)
    padded = jnp.concatenate([zeros_pad, key_piece, zeros_pad], axis=0)
    for slot_index in range(slot_count):
        lead = first_key - slot_start[slot_index]
        dest_first = jnp.clip(lead, 0, longest - window)
        source_first = jnp.clip(window + dest_first - lead, 0, piece_rows + window)
        shifted = lax.dynamic_slice_in_dim(padded, source_first, window, 0)
        current = lax.dynamic_slice(
            landed, (slot_index, dest_first, 0), (1, window, landed.shape[2])
        )[0]
        dest_rows = dest_first + jnp.arange(window, dtype=jnp.int32)
        source_rows = dest_rows - lead
        valid = (
            (dest_rows < slot_length[slot_index]) & (source_rows >= 0) & (source_rows < piece_rows)
        )
        blended = jnp.where(valid[:, None], shifted, current)
        landed = lax.dynamic_update_slice(landed, blended[None], (slot_index, dest_first, 0))
    return landed


def decode_core(
    absorbed,
    query_rope,
    resident,
    resident_valid,
    prompts,
    prompt_valid,
    slot_row,
    fresh_keys,
    fresh_valid,
    value_heads,
    score_scale,
):
    latent_dim = value_heads.shape[0]
    row_count = absorbed.shape[0]
    onehot = slot_row[:, None] == jnp.arange(row_count, dtype=jnp.int32)[None, :]
    picker = onehot.astype(jnp.bfloat16)
    slot_latent = product("kr,rhl->khl", picker, absorbed).astype(jnp.bfloat16)
    slot_rope = product("kr,rhe->khe", picker, query_rope).astype(jnp.bfloat16)
    res_scores = (
        product("rhl,rcl->rhc", absorbed, resident[..., :latent_dim])
        + product("rhe,rce->rhc", query_rope, resident[..., latent_dim:])
    ) * score_scale
    fresh_scores = (
        product("rhl,rtl->rht", absorbed, fresh_keys[..., :latent_dim])
        + product("rhe,rte->rht", query_rope, fresh_keys[..., latent_dim:])
    ) * score_scale
    slot_scores = (
        product("khl,kpl->khp", slot_latent, prompts[..., :latent_dim])
        + product("khe,kpe->khp", slot_rope, prompts[..., latent_dim:])
    ) * score_scale
    res_mask = resident_valid[:, None, :]
    fresh_mask = fresh_valid[:, None, :]
    slot_mask = prompt_valid[:, None, :]
    res_best = jnp.max(jnp.where(res_mask, res_scores, -jnp.inf), axis=2)
    fresh_best = jnp.max(jnp.where(fresh_mask, fresh_scores, -jnp.inf), axis=2)
    slot_best = jnp.max(jnp.where(slot_mask, slot_scores, -jnp.inf), axis=2)
    routed = onehot[:, :, None]
    slot_best_rows = jnp.max(jnp.where(routed, slot_best[:, None, :], -jnp.inf), axis=0)
    row_best = jnp.maximum(jnp.maximum(res_best, fresh_best), slot_best_rows)
    occupied = jnp.any(onehot, axis=1)[:, None]
    slot_shift = jnp.where(
        occupied, jnp.max(jnp.where(routed, row_best[None, :, :], -jnp.inf), axis=1), 0.0
    )
    res_weights = jnp.where(res_mask, jnp.exp(res_scores - row_best[:, :, None]), 0.0)
    fresh_weights = jnp.where(fresh_mask, jnp.exp(fresh_scores - row_best[:, :, None]), 0.0)
    slot_weights = jnp.where(slot_mask, jnp.exp(slot_scores - slot_shift[:, :, None]), 0.0)
    slot_total = jnp.sum(jnp.where(routed, jnp.sum(slot_weights, axis=2)[:, None, :], 0.0), axis=0)
    weight_sum = jnp.sum(res_weights, axis=2) + jnp.sum(fresh_weights, axis=2) + slot_total
    slot_accum = product(
        "khp,kpl->khl", slot_weights.astype(jnp.bfloat16), prompts[..., :latent_dim]
    )
    accumulated = product(
        "rhc,rcl->rhl", res_weights.astype(jnp.bfloat16), resident[..., :latent_dim]
    )
    accumulated = accumulated + product(
        "rht,rtl->rhl", fresh_weights.astype(jnp.bfloat16), fresh_keys[..., :latent_dim]
    )
    accumulated = accumulated + jnp.sum(
        jnp.where(routed[..., None], slot_accum[:, None], 0.0), axis=0
    )
    latent_out = (accumulated / weight_sum[:, :, None]).astype(jnp.bfloat16)
    return (
        product("rhl,lhv->rhv", latent_out, value_heads).astype(jnp.bfloat16).reshape(row_count, -1)
    )


def on_device(
    prefill_query,
    span_latent,
    prompt_lengths,
    key_weight,
    value_weight,
    placement,
    resident_cache,
    resident_lengths,
    decode_query,
    decode_latent,
    out_weight,
):
    local_tokens = span_latent.shape[0]
    latent_width = span_latent.shape[1]
    latent_dim = key_weight.shape[0]
    rope_dim = latent_width - latent_dim
    head_count = key_weight.shape[1] // NOPE
    score_scale = 1.0 / math.sqrt(NOPE + rope_dim)
    queries = prefill_query.reshape(local_tokens, head_count, NOPE + rope_dim)
    query_plain = queries[:, :, :NOPE]
    query_rope = queries[:, :, NOPE:]
    request_ends = jnp.cumsum(prompt_lengths)
    group_index = lax.axis_index("ctx")
    first_token = group_index * local_tokens
    query_pos = first_token + jnp.arange(local_tokens, dtype=jnp.int32)
    query_seg = segment_ids(query_pos, request_ends)
    initial = (
        jnp.full((local_tokens, head_count), -1e30, jnp.float32),
        jnp.zeros((local_tokens, head_count), jnp.float32),
        jnp.zeros((local_tokens, head_count, VHEAD), jnp.float32),
    )
    local_rows = resident_cache.shape[0]
    prompt_max = local_tokens * lax.axis_size("ctx") * 5 // 8
    request_starts = request_ends - prompt_lengths
    arriving = placement // local_rows == group_index
    slot_rank = jnp.cumsum(arriving.astype(jnp.int32)) - 1
    chosen = (
        arriving[None, :] & (slot_rank[None, :] == jnp.arange(NEW_DEV, dtype=jnp.int32)[:, None])
    ).astype(jnp.int32)
    present = jnp.sum(chosen, axis=1) > 0
    slot_start = jnp.sum(chosen * request_starts[None, :], axis=1)
    slot_length = jnp.sum(chosen * prompt_lengths[None, :], axis=1)
    slot_row = jnp.where(present, jnp.sum(chosen * (placement % local_rows)[None, :], axis=1), -1)
    offsets = jnp.arange(prompt_max, dtype=jnp.int32)
    slot_valid = offsets[None, :] < slot_length[:, None]
    empty_landed = jnp.zeros((NEW_DEV, prompt_max, latent_width), jnp.bfloat16)
    landed = None
    key_piece = lax.all_gather(span_latent, "ctx", axis=0, tiled=True)
    key_count = key_piece.shape[0]
    key_pos = jnp.arange(key_count, dtype=jnp.int32)
    key_seg = segment_ids(key_pos, request_ends)
    key_plain = jnp.dot(
        key_piece[:, :latent_dim], key_weight, preferred_element_type=jnp.float32
    ).astype(jnp.bfloat16)
    value_rows = jnp.dot(
        key_piece[:, :latent_dim], value_weight, preferred_element_type=jnp.float32
    ).astype(jnp.bfloat16)
    key_plain, value_rows = (key_plain, value_rows)
    key_plain, key_rope, value_rows = (key_plain, key_piece[:, latent_dim:], value_rows)
    attention_state = attend_block(
        initial,
        query_plain,
        query_rope,
        key_plain.reshape(key_count, head_count, NOPE),
        key_rope,
        value_rows.reshape(key_count, head_count, VHEAD),
        query_pos,
        query_seg,
        key_pos,
        key_seg,
        score_scale,
    )
    attention_state, landed = (attention_state, empty_landed)
    running_max, weight_sum, accumulated = attention_state
    landed = None
    prefill_out = (
        (accumulated / weight_sum[:, :, None])
        .astype(jnp.bfloat16)
        .reshape(local_tokens, head_count * VHEAD)
    )
    landed = land_piece(
        empty_landed,
        lax.all_gather(span_latent, "ctx", axis=0, tiled=True),
        jnp.int32(0),
        slot_start,
        slot_length,
    )
    step_count = decode_query.shape[1]
    decode_heads = decode_query.reshape(local_rows, step_count, head_count, NOPE + rope_dim)
    absorbed = product(
        "rshn,lhn->rshl", decode_heads[..., :NOPE], key_weight.reshape(latent_dim, head_count, NOPE)
    ).astype(jnp.bfloat16)
    global_rows = group_index * local_rows + jnp.arange(local_rows, dtype=jnp.int32)
    replaced = jnp.any(placement[None, :] == global_rows[:, None], axis=1)
    resident_valid = (
        jnp.arange(resident_cache.shape[1], dtype=jnp.int32)[None, :] < resident_lengths[:, None]
    ) & jnp.logical_not(replaced)[:, None]
    value_heads = value_weight.reshape(latent_dim, head_count, VHEAD)
    results = []
    for step_index in range(step_count):
        fresh_valid = jnp.broadcast_to(
            jnp.arange(step_count)[None, :] <= step_index, (local_rows, step_count)
        )
        results.append(
            decode_core(
                absorbed[:, step_index],
                decode_heads[:, step_index, :, NOPE:],
                resident_cache,
                resident_valid,
                landed,
                slot_valid,
                slot_row,
                decode_latent,
                fresh_valid,
                value_heads,
                score_scale,
            )
        )
    head_mixed = jnp.stack(results, axis=1)
    decode_out = lax.psum_scatter(
        product("rsk,kd->rsd", head_mixed, out_weight).astype(jnp.bfloat16),
        "tp",
        scatter_dimension=0,
        tiled=True,
    )
    return (prefill_out, decode_out)


def solution(mesh):
    placed = (
        P("ctx", "tp"),
        P("ctx", None),
        P(),
        P(None, "tp"),
        P(None, "tp"),
        P(),
        P("ctx", None, None),
        P("ctx"),
        P("ctx", None, "tp"),
        P("ctx", None, None),
        P("tp", None),
    )
    return jax.shard_map(
        on_device,
        mesh=mesh,
        in_specs=placed,
        out_specs=(P("ctx", "tp"), P(("ctx", "tp"), None, None)),
        check_vma=False,
    )
```

profile of v0, /device:TPU:1, one launch (start us, length us, event | category | flops | bytes accessed | tf_op | source)
XLA Modules:
  0.0 215.5 jit_solution(12574489078719473334)
XLA Ops:
  15.4 1.5 copy.175
  17.7 1.4 copy.122
  19.1 1.3 dynamic-slice
  21.1 1.4 fusion.121
  22.5 1.4 fusion.123
  24.1 1.3 fusion.141
  29.1 2.1 select_reduce_fusion.8
  32.1 2.1 select_reduce_fusion.7
  37.0 1.9 fusion.62
  38.9 1.9 select_reduce_fusion.6
  41.6 1.9 fusion.14
  43.5 17.3 %all-gather.2.cloned.1.call-done = bf16[4096,576]{0,1:T(8,128)(2,1)} async-done(((bf16[256,576]{0,1:T(8,128)(2,1)}), bf16[4096,576]{0,1:T(8,128)(2,1)}) %all-gather.2.cloned.1.call-update) | async-done | bytes 4718608 | tf_op jit(solution)/shard_map/all_gather | solution.py:190
  61.0 4.2 %pad_maximum_fusion = bf16[9216,576]{0,1:T(8,128)(2,1)S(1)} fusion(bf16[2560,576]{0,1:T(8,128)(2,1)S(1)} %broadcast.266, bf16[4096,576]{0,1:T(8,128)(2,1)} %all-gather.2.cloned.1.call-done), kind=kLoop, calls=%fused_computation.12 | loop fusion | flops 31850496 | bytes 18284544 | tf_op jit(solution)/shard_map/concatenate | solution.py:56
  65.3 4.3 %select_bitcast_fusion = (bf16[1,2560,576]{1,2,0:T(8,128)(2,1)S(1)}, bf16[1,2560,576]{1,2,0:T(8,128)(2,1)S(1)}) fusion(bf16[9216,576]{0,1:T(8,128)(2,1)S(1)} %pad_maximum_fusion, s32[]{:T(128)S(6)} %min.16, pred[2560]{0:T(1024)(128)(4,1)S(1)} %copy-done.20, s32[]{:T(128)S(6)} %min.14, pred[2560]{0:T(1024)(128)(4,1)S(1)} %copy-done.19), kind=kLoop, calls=%fused_computation.27 | loop fusion | flops 2949120 | bytes 11801608 | tf_op jit(solution)/shard_map/broadcast_in_dim | solution.py:71
  74.2 1.3 copy.137
  75.5 1.3 maximum_maximum_fusion.1
  76.9 1.4 copy.138
  79.1 3.4 %fusion.107 = f32[2,8,2560]{2,1,0:T(8,128)S(1)} fusion(bf16[2,2560,512]{1,2,0:T(8,128)(2,1)} %copy-done.1, bf16[2,8,512]{2,0,1:T(2,128)(2,1)} %convolution_convert_fusion.5), kind=kOutput, calls=%fused_computation.132 | convolution fusion | flops 41943040 | bytes 5423104 | tf_op jit(solution)/shard_map/khl,kpl->khp/dot_general | solution.py:14
  82.5 4.2 %fusion.21 = f32[16,8,512]{2,1,0:T(8,128)} fusion(bf16[16,256,576]{1,2,0:T(8,128)(2,1)} %param.17, f32[16,8,256]{2,1,0:T(8,128)S(1)} %copy-done.5, f32[16,8]{1,0:T(8,128)S(1)} %copy-done.9, pred[16,256]{1,0:T(8,128)(4,1)S(1)} %fusion.111), kind=kOutput, calls=%fused_computation.31 | convolution fusion | flops 33652736 | bytes 4592128 | tf_op jit(solution)/shard_map/rhc,rcl->rhl/dot_general | solution.py:14
  86.7 4.1 %fusion.79 = (f32[16,8]{1,0:T(8,128)}, f32[16,8]{1,0:T(8,128)}, f32[16,8,256]{2,1,0:T(8,128)}) fusion(f32[16,8,256]{2,1,0:T(8,128)S(1)} %copy-done.5, f32[16,8]{1,0:T(8,128)S(1)} %copy-done.9, pred[16,256]{1,0:T(8,128)(4,1)S(1)} %fusion.111, f32[16,8,256]{2,1,0:T(8,128)S(1)} %copy-done.8, bf16[16,256,576]{1,2,0:T(8,128)(2,1)} %param.17, ...), kind=kOutput, calls=%fused_computation.105 | convolution fusion | flops 33783552 | bytes 4724224 | tf_op jit(solution)/shard_map/rhl,rcl->rhc/dot_general | solution.py:14
  91.0 2.1 fusion.85
  96.4 4.0 %fusion.83 = f32[2,8,512]{2,1,0:T(8,128)S(1)} fusion(bf16[2,2560,512]{1,2,0:T(8,128)(2,1)} %copy-done.1, f32[2,8,2560]{2,1,0:T(8,128)} %get-tuple-element.46, f32[2,8]{1,0:T(2,128)S(1)} %broadcast_select_fusion, pred[2,2560]{1,0:T(4,128)(4,1)S(1)} %iota_compare_fusion.2), kind=kOutput, calls=%fused_computation.109 | convolution fusion | flops 42065920 | bytes 5444672 | tf_op jit(solution)/shard_map/khp,kpl->khl/dot_general | solution.py:14
  102.3 4.2 %fusion.25 = f32[16,8,512]{2,1,0:T(8,128)} fusion(bf16[16,256,576]{1,2,0:T(8,128)(2,1)} %param.17, f32[16,8,256]{2,1,0:T(8,128)} %get-tuple-element.47, f32[16,8]{1,0:T(8,128)S(1)} %maximum_maximum_fusion, pred[16,256]{1,0:T(8,128)(4,1)S(1)} %fusion.111), kind=kOutput, calls=%fused_computation.35 | convolution fusion | flops 33652736 | bytes 4592128 | tf_op jit(solution)/shard_map/rhc,rcl->rhl/dot_general | solution.py:14
  106.8 1.3 fusion.35
  108.8 1.3 fusion.36
  110.4 8.6 %fusion.10 = bf16[16,2,7168]{2,0,1:T(8,128)(2,1)} fusion(bf16[1024,7168]{1,0:T(8,128)(2,1)} %param.21, bf16[16,1,1024]{2,0,1:T(8,128)(2,1)S(1)} %stack_reshape.7, bf16[16,1,1024]{2,0,1:T(8,128)(2,1)S(1)} %stack_reshape.6), kind=kOutput, calls=%fused_computation.13 | convolution fusion | flops 470024192 | bytes 15204352 | tf_op jit(solution)/shard_map/rsk,kd->rsd/dot_general | solution.py:14
  119.0 10.2 %convolution_convert_fusion = bf16[4096,1024]{0,1:T(8,128)(2,1)} fusion(bf16[512,1024]{1,0:T(8,128)(2,1)} %param.14, bf16[4096,576]{0,1:T(8,128)(2,1)} %all-gather.2.cloned.1.call-done), kind=kOutput, calls=%fused_computation.14 | convolution fusion | flops 4299161600 | bytes 13631488 | tf_op jit(solution)/shard_map/dot_general | solution.py:194
  129.2 15.4 %fusion.60 = f32[8,4096,256]{2,1,0:T(8,128)} fusion(bf16[4096,8,128]{0,2,1:T(8,128)(2,1)} %bitcast.101, bf16[256,8,192]{0,2,1:T(8,128)(2,1)S(1)} %bitcast.102), kind=kOutput, calls=%fused_computation.72 | convolution fusion | flops 2147483648 | bytes 42467328 | tf_op jit(solution)/shard_map/qhn,khn->qhk/dot_general | solution.py:14
  144.6 21.8 %select_reduce_fusion = (f32[256,8]{0,1:T(8,128)S(1)}, f32[256,8,4096]{0,2,1:T(8,128)}) fusion(pred[256,4096]{0,1:T(8,128)(4,1)S(1)} %fusion.14, bf16[4096,576]{0,1:T(8,128)(2,1)} %all-gather.2.cloned.1.call-done, bf16[256,8,192]{0,2,1:T(8,128)(2,1)S(1)} %bitcast.103, f32[8,4096,256]{2,1,0:T(8,128)} %fusion.60), kind=kOutput, calls=%fused_computation.3 | convolution fusion | flops 1107294208 | bytes 68952064 | tf_op jit(solution)/shard_map/qhe,ke->qhk/dot_general | solution.py:14
  166.4 13.9 %fusion.1 = f32[256,8]{0,1:T(8,128)S(1)} fusion(f32[256,8,4096]{0,2,1:T(8,128)} %get-tuple-element.39, f32[256,8]{0,1:T(8,128)S(1)} %broadcast_maximum_fusion, pred[256,4096]{0,1:T(8,128)(4,1)S(1)} %fusion.14), kind=kLoop, calls=%fused_computation.4 | loop fusion | flops 25163776 | bytes 34619392 | tf_op jit(solution)/shard_map/reduce_sum | solution.py:45
  180.3 8.9 %convolution_convert_fusion.1 = bf16[4096,1024]{0,1:T(8,128)(2,1)} fusion(bf16[512,1024]{1,0:T(8,128)(2,1)S(1)} %copy-done, bf16[4096,576]{0,1:T(8,128)(2,1)} %all-gather.2.cloned.1.call-done), kind=kOutput, calls=%fused_computation.15 | convolution fusion | flops 4299161600 | bytes 13631488 | tf_op jit(solution)/shard_map/dot_general | solution.py:197
  189.2 16.7 %divide_convert_fusion = bf16[256,8,128]{0,2,1:T(8,128)(2,1)S(1)} fusion(bf16[4096,8,128]{0,2,1:T(8,128)(2,1)} %bitcast.110, f32[256,8,4096]{0,2,1:T(8,128)} %get-tuple-element.39, f32[256,8]{0,1:T(8,128)S(1)} %broadcast_maximum_fusion, pred[256,4096]{0,1:T(8,128)(4,1)S(1)} %fusion.14, f32[256,8]{0,1:T(8,128)S(1)} %fusion.1), kind=kOutput, calls=%fused_computation.67 | convolution fusion | flops 2173173760 | bytes 43532288 | tf_op jit(solution)/shard_map/qhk,khv->qhv/dot_general | solution.py:14
  (137 shorter events, 30.9 us)
Async XLA Ops:
  7.2 100.9 %copy-start = (bf16[512,1024]{1,0:T(8,128)(2,1)S(1)}, bf16[512,1024]{1,0:T(8,128)(2,1)}, u32[]{:S(2)}) copy-start(bf16[512,1024]{1,0:T(8,128)(2,1)} %param.15) | copy-start | bytes 3145732
  7.2 53.6 %all-gather.2.cloned.1.call-start = ((), (), s32[]{:S(2)}) async-start(), calls=%async_computation | async-start | bytes 5013504 | tf_op jit(solution)/shard_map/all_gather | solution.py:190
  7.9 199.1 %all-reduce.3.cloned.1.call-start = ((), (), s32[]{:S(2)}) async-start(), calls=%async_computation.1 | async-start | bytes 917504
  21.0 17.9 %copy-start.2 = (bf16[16,256,576]{1,2,0:T(8,128)(2,1)S(1)}, bf16[16,256,576]{1,2,0:T(8,128)(2,1)}, u32[]{:S(2)}) copy-start(bf16[16,256,576]{1,2,0:T(8,128)(2,1)} %param.17) | copy-start | bytes 14155780
  21.0 17.9 %copy-start.28 = (pred[2]{0:T(512)(128)(4,1)}, pred[2]{0:T(512)(128)(4,1)S(1)}, u32[]{:S(2)}) copy-start(pred[2]{0:T(512)(128)(4,1)S(1)} %iota_compare_fusion.6) | copy-start | bytes 10
  21.0 17.9 %copy-start.26 = (pred[2]{0:T(512)(128)(4,1)}, pred[2]{0:T(512)(128)(4,1)S(1)}, u32[]{:S(2)}) copy-start(pred[2]{0:T(512)(128)(4,1)S(1)} %iota_compare_fusion.5) | copy-start | bytes 10
  28.1 32.9 %copy-start.6 = (bf16[16,8,512]{2,0,1:T(8,128)(2,1)}, bf16[16,8,512]{2,0,1:T(8,128)(2,1)S(1)}, u32[]{:S(2)}) copy-start(bf16[16,8,512]{2,0,1:T(8,128)(2,1)S(1)} %get-tuple-element.28) | copy-start | bytes 393220
  61.0 4.3 %copy-start.19 = (pred[2560]{0:T(1024)(128)(4,1)S(1)}, pred[2560]{0:T(1024)(128)(4,1)}, u32[]{:S(2)}) copy-start(pred[2560]{0:T(1024)(128)(4,1)} %fusion.121) | copy-start | bytes 7684
  61.0 4.3 %copy-start.20 = (pred[2560]{0:T(1024)(128)(4,1)S(1)}, pred[2560]{0:T(1024)(128)(4,1)}, u32[]{:S(2)}) copy-start(pred[2560]{0:T(1024)(128)(4,1)} %fusion.123) | copy-start | bytes 7684
  70.4 2.3 %copy-start.1 = (bf16[2,2560,512]{1,2,0:T(8,128)(2,1)}, bf16[2,2560,512]{1,2,0:T(8,128)(2,1)S(1)}, u32[]{:S(2)}) copy-start(bf16[2,2560,512]{1,2,0:T(8,128)(2,1)S(1)} %fusion.13) | copy-start | bytes 15728644
  70.4 2.3 %copy-start.23 = (bf16[2,8,64]{2,0,1:T(2,128)(2,1)S(1)}, bf16[2,8,64]{2,0,1:T(2,128)(2,1)}, u32[]{:S(2)}) copy-start(bf16[2,8,64]{2,0,1:T(2,128)(2,1)} %convolution_convert_fusion.8) | copy-start | bytes 6148
  70.4 3.2 %copy-start.14 = (pred[2,16]{1,0:T(4,128)(4,1)S(1)}, pred[2,16]{1,0:T(4,128)(4,1)}, u32[]{:S(2)}) copy-start(pred[2,16]{1,0:T(4,128)(4,1)} %get-tuple-element.33) | copy-start | bytes 100
  78.2 4.3 %copy-start.5 = (f32[16,8,256]{2,1,0:T(8,128)S(1)}, f32[16,8,256]{2,1,0:T(8,128)}, u32[]{:S(2)}) copy-start(f32[16,8,256]{2,1,0:T(8,128)} %get-tuple-element.43) | copy-start | bytes 393220
  78.2 4.3 %copy-start.9 = (f32[16,8]{1,0:T(8,128)S(1)}, f32[16,8]{1,0:T(8,128)}, u32[]{:S(2)}) copy-start(f32[16,8]{1,0:T(8,128)} %maximum_maximum_fusion.1) | copy-start | bytes 1540
  78.2 8.5 %copy-start.7 = (bf16[16,8,512]{2,0,1:T(8,128)(2,1)S(1)}, bf16[16,8,512]{2,0,1:T(8,128)(2,1)}, u32[]{:S(2)}) copy-start(bf16[16,8,512]{2,0,1:T(8,128)(2,1)} %copy-done.6) | copy-start | bytes 393220
  78.2 8.5 %copy-start.8 = (f32[16,8,256]{2,1,0:T(8,128)S(1)}, f32[16,8,256]{2,1,0:T(8,128)}, u32[]{:S(2)}) copy-start(f32[16,8,256]{2,1,0:T(8,128)} %fusion.62) | copy-start | bytes 393220
  79.1 11.9 %slice-start = ((s8[5242880]{0:T(1024)(128)(4,1)}), s8[4194304]{0:T(1024)(128)(4,1)S(1)}, s32[]{:S(2)}) async-start(s8[5242880]{0:T(1024)(128)(4,1)} %bitcast.99), calls=%async_computation.2 | async-start | bytes 8388608
  82.5 8.4 %copy-start.25 = (pred[2]{0:T(512)(128)(4,1)S(1)}, pred[2]{0:T(512)(128)(4,1)}, u32[]{:S(2)}) copy-start(pred[2]{0:T(512)(128)(4,1)} %get-tuple-element.32) | copy-start | bytes 10
  82.5 8.5 %copy-start.3 = (f32[2,8,2560]{2,1,0:T(8,128)S(1)}, f32[2,8,2560]{2,1,0:T(8,128)}, u32[]{:S(2)}) copy-start(f32[2,8,2560]{2,1,0:T(8,128)} %get-tuple-element.41) | copy-start | bytes 491524
  82.5 8.5 %slice-start.1 = ((s8[5242880]{0:T(1024)(128)(4,1)}), s8[1048576]{0:T(1024)(128)(4,1)S(1)}, s32[]{:S(2)}) async-start(s8[5242880]{0:T(1024)(128)(4,1)} %bitcast.99), calls=%async_computation.3 | async-start | bytes 2097152
  86.7 6.3 %copy-start.22 = (bf16[2,8,64]{2,0,1:T(2,128)(2,1)S(1)}, bf16[2,8,64]{2,0,1:T(2,128)(2,1)}, u32[]{:S(2)}) copy-start(bf16[2,8,64]{2,0,1:T(2,128)(2,1)} %convolution_convert_fusion.7) | copy-start | bytes 6148
  86.7 7.2 %copy-start.15 = (pred[2,16]{1,0:T(4,128)(4,1)S(1)}, pred[2,16]{1,0:T(4,128)(4,1)}, u32[]{:S(2)}) copy-start(pred[2,16]{1,0:T(4,128)(4,1)} %get-tuple-element.33) | copy-start | bytes 100
  94.0 6.5 %copy-start.4 = (f32[2,8,2560]{2,1,0:T(8,128)S(1)}, f32[2,8,2560]{2,1,0:T(8,128)}, u32[]{:S(2)}) copy-start(f32[2,8,2560]{2,1,0:T(8,128)} %get-tuple-element.46) | copy-start | bytes 491524
  94.0 12.6 %copy-start.10 = (f32[16,8]{1,0:T(8,128)S(1)}, f32[16,8]{1,0:T(8,128)}, u32[]{:S(2)}) copy-start(f32[16,8]{1,0:T(8,128)} %maximum_maximum_fusion.1) | copy-start | bytes 1540
  94.0 12.6 %copy-start.18 = (f32[16,8,2]{1,2,0:T(2,128)S(1)}, f32[16,8,2]{1,2,0:T(2,128)}, u32[]{:S(2)}) copy-start(f32[16,8,2]{1,2,0:T(2,128)} %get-tuple-element.45) | copy-start | bytes 3076
  94.0 12.6 %copy-start.29 = (pred[2]{0:T(512)(128)(4,1)S(1)}, pred[2]{0:T(512)(128)(4,1)}, u32[]{:S(2)}) copy-start(pred[2]{0:T(512)(128)(4,1)} %copy-done.28) | copy-start | bytes 10
  94.1 12.5 %copy-start.11 = (f32[2,8,512]{2,1,0:T(8,128)S(1)}, f32[2,8,512]{2,1,0:T(8,128)}, u32[]{:S(2)}) copy-start(f32[2,8,512]{2,1,0:T(8,128)} %fusion.85) | copy-start | bytes 98308
  94.1 12.5 %copy-start.16 = (pred[2,16]{1,0:T(4,128)(4,1)S(1)}, pred[2,16]{1,0:T(4,128)(4,1)}, u32[]{:S(2)}) copy-start(pred[2,16]{1,0:T(4,128)(4,1)} %get-tuple-element.33) | copy-start | bytes 100
  96.4 10.4 %copy-start.13 = (f32[16,8]{1,0:T(8,128)S(1)}, f32[16,8]{1,0:T(8,128)}, u32[]{:S(2)}) copy-start(f32[16,8]{1,0:T(8,128)} %get-tuple-element.14) | copy-start | bytes 1540
  100.4 8.1 %copy-start.17 = (f32[16,8,2]{1,2,0:T(2,128)S(1)}, f32[16,8,2]{1,2,0:T(2,128)}, u32[]{:S(2)}) copy-start(f32[16,8,2]{1,2,0:T(2,128)} %get-tuple-element.49) | copy-start | bytes 3076
  100.4 8.1 %copy-start.27 = (pred[2]{0:T(512)(128)(4,1)S(1)}, pred[2]{0:T(512)(128)(4,1)}, u32[]{:S(2)}) copy-start(pred[2]{0:T(512)(128)(4,1)} %copy-done.26) | copy-start | bytes 10
  101.2 7.4 %copy-start.24 = (f32[2,8]{1,0:T(2,128)S(1)}, f32[2,8]{1,0:T(2,128)}, u32[]{:S(2)}) copy-start(f32[2,8]{1,0:T(2,128)} %fusion.69) | copy-start | bytes 196
  (2 other events, 1.3 us)
Sparse Core Ops, SparseCore 0:
  9.6 51.1 all-gather.1
  119.1 79.3 all-reduce.2
where the time goes:
time: 217 us; the launch traced here: 215 us
  matrix products  124 us (57%)
  other arithmetic  42.8 us (20%)
  waiting for transfers between devices  18 us (8%)
  between operations  16.6 us (8%)
  local copies, waits for them, and re-layouts  13.9 us (6%)
    dot_general x29, matrix products, product(): return jnp.einsum(form, left, right, preferred_element_type=jnp.float32)  105 us
    all_gather x1, waiting for transfers between devices, on_device(): key_piece = lax.all_gather(span_latent, 'ctx', axis=0, tiled=True)  17.3 us
    reduce_sum x1, other arithmetic, attend_block(): weight_sum = jnp.sum(weights, axis=2)  13.9 us
    dot_general x1, matrix products, on_device(): jnp.dot(key_piece[:, :latent_dim], key_weight, preferred_element_type=jnp...  10.2 us
    unnamed x71, local copies, waits for them, and re-layouts  9.9 us
    dot_general x1, matrix products, on_device(): jnp.dot(key_piece[:, :latent_dim], value_weight, preferred_element_type=j...  8.94 us
  transfers between devices with their start and end apart: 2, of which 1 were waited for; matrix products, arithmetic and copies ran while one was open for 56% of the time, Pallas kernels for 0%

commit v1 on v0

v1 whole, which is shorter than its diff:
```python
import functools
import math

import jax
import jax.numpy as jnp
from jax import lax
from jax.experimental import pallas as pl
from jax.experimental.pallas import tpu as pltpu
from jax.sharding import PartitionSpec as P

MESH = pl.DeviceIdType.MESH
NOPE = 128
ROPE = 64
LATENT = 512
WIDTH = LATENT + ROPE
BLOCK = 256
N_CTX = 16
N_TP = 8
HEADS = 8
ROWS = 16
STEPS = 2
NREQ = 8
BIG = 1e30
FACTOR = math.log2(math.e) / math.sqrt(NOPE + ROPE)
F32 = jnp.float32
BF16 = jnp.bfloat16
MIB = 1 << 20


def mm(left, right):
    return lax.dot_general(left, right, (((1,), (0,)), ((), ())), preferred_element_type=F32)


def mm_nt(left, right):
    return lax.dot_general(left, right, (((1,), (1,)), ((), ())), preferred_element_type=F32)


def iota(shape, dim):
    return lax.broadcasted_iota(jnp.int32, shape, dim)


def request_table(lens_ref):
    starts, ends, total = [], [], jnp.int32(0)
    for j in range(NREQ):
        starts.append(total)
        total = total + lens_ref[j]
        ends.append(total)
    return starts, ends


def spread(index, values, other):
    out = jnp.full(index.shape, other, jnp.int32)
    for j, value in enumerate(values):
        out = jnp.where(index == j, value, out)
    return out


def chip_parts():
    ctx = lax.axis_index("ctx")
    tp = lax.axis_index("tp")
    return ctx, tp


def gather_kernel(own_ref, all_ref, send_sem, recv_sem, copy_sem):
    ctx, tp = chip_parts()
    barrier = pltpu.get_barrier_semaphore()
    for d in range(1, N_CTX):
        peer = lax.rem(ctx + d, N_CTX)
        pl.semaphore_signal(barrier, inc=1, device_id=(peer, tp), device_id_type=MESH)
    pl.semaphore_wait(barrier, N_CTX - 1)
    mine = all_ref.at[pl.ds(pl.multiple_of(ctx * WIDTH, 64), WIDTH)]
    local = pltpu.make_async_copy(own_ref, mine, copy_sem)
    local.start()

    def copy_to(d):
        return pltpu.make_async_remote_copy(
            src_ref=own_ref,
            dst_ref=mine,
            send_sem=send_sem.at[d],
            recv_sem=recv_sem.at[d],
            device_id=(lax.rem(ctx + d, N_CTX), tp),
            device_id_type=MESH,
        )

    copies = [copy_to(d) for d in range(1, N_CTX)]
    for c in copies:
        c.start()
    local.wait()
    for d in range(1, N_CTX):
        source = lax.rem(ctx - d + N_CTX, N_CTX)
        theirs = all_ref.at[pl.ds(pl.multiple_of(source * WIDTH, 64), WIDTH)]
        pltpu.make_async_copy(own_ref, theirs, recv_sem.at[d]).wait()
    for c in copies:
        c.wait_send()


def gather(latent_t):
    return pl.pallas_call(
        gather_kernel,
        out_shape=jax.ShapeDtypeStruct((N_CTX * WIDTH, BLOCK), BF16),
        in_specs=[pl.BlockSpec(memory_space=pltpu.VMEM)],
        out_specs=pl.BlockSpec(memory_space=pltpu.VMEM),
        scratch_shapes=[
            pltpu.SemaphoreType.DMA((N_CTX,)),
            pltpu.SemaphoreType.DMA((N_CTX,)),
            pltpu.SemaphoreType.DMA,
        ],
        compiler_params=pltpu.CompilerParams(collective_id=0, has_side_effects=True, vmem_limit_bytes=60 * MIB),
        name="gather",
    )(latent_t)


def prepare_weights(wk_ref, wv_ref, wkt, wvt):
    wkt[...] = wk_ref[...].T
    wvt[...] = wv_ref[...].T


def prepare_queries(me, q_ref, starts, ends, qs):
    lane = iota((BLOCK, 256), 1)
    pos = me * BLOCK + iota((BLOCK, 256), 0)
    for odd in range(2):
        slot = lane if odd else lane - 192
        first = spread(slot, starts, 1 << 30)
        last = spread(slot, ends, -1)
        hot = ((pos >= first) & (pos < last)).astype(F32)
        spare = lane < 64 if odd else lane >= 192
        for pair in range(HEADS // 2):
            base = pair * 384 + odd * 128
            window = q_ref[:, base : base + 256].astype(F32)
            qs[2 * pair + odd] = jnp.where(spare, hot, window).astype(BF16)


def latent_rows(g_ref, block, first, count):
    return g_ref[pl.ds(pl.multiple_of(block * WIDTH + first, 64), count), :]


def attend_pair(pair, causal, me, g_ref, starts, ends, wkt, wvt, qs, kt, vt, best, acc):
    ropes = []
    for half in range(2):
        lat = latent_rows(g_ref, 2 * pair + half, 0, LATENT)
        cols = slice(half * BLOCK, (half + 1) * BLOCK)
        kt[:, cols] = mm(wkt[...], lat).astype(BF16)
        vt[:, cols] = mm(wvt[...], lat).astype(BF16)
        ropes.append(latent_rows(g_ref, 2 * pair + half, LATENT, ROPE))
    rope = jnp.concatenate(ropes, axis=1)
    keys = 2 * BLOCK
    slot = iota((ROPE, keys), 0)
    key_pos = pair * keys + iota((ROPE, keys), 1)
    outside = (slot < NREQ) & ((key_pos < spread(slot, starts, 0)) | (key_pos >= spread(slot, ends, 0)))
    aug = jnp.where(outside, -BIG, 0.0).astype(BF16)
    ones = jnp.ones((NOPE, keys), BF16)
    for h in range(HEADS):
        head = slice(h * NOPE, (h + 1) * NOPE)
        parts = [aug, kt[head, :], rope] if h % 2 else [kt[head, :], rope, aug]
        s = mm(qs[h], jnp.concatenate(parts, axis=0))
        if causal:
            ahead = pair * keys + iota((BLOCK, keys), 1) > me * BLOCK + iota((BLOCK, keys), 0)
            s = jnp.where(ahead, -BIG, s)
        block_best = jnp.max(s, axis=1, keepdims=True) * FACTOR
        values = jnp.concatenate([vt[head, :], ones], axis=0)
        if causal:
            new_best = jnp.broadcast_to(block_best, (BLOCK, 128))
        else:
            new_best = jnp.maximum(best[h], block_best)
        p = jnp.exp2(s * FACTOR - jnp.concatenate([new_best] * 4, axis=1)).astype(BF16)
        gained = mm_nt(p, values)
        if causal:
            acc[h] = gained
        else:
            keep = jnp.exp2(best[h] - new_best)
            acc[h] = acc[h] * jnp.concatenate([keep] * 2, axis=1) + gained
        best[h] = new_best


def finish_prefill(acc, out_ref):
    for h in range(HEADS):
        out_ref[:, h * NOPE : (h + 1) * NOPE] = (acc[h][:, :NOPE] / acc[h][:, NOPE:]).astype(BF16)


def to_row_major(index):
    return (index % HEADS) * (ROWS * STEPS) + index // HEADS


def hot_matrix(condition):
    return condition.astype(F32).astype(BF16)


def decode_queries(dq_ref, wkt, qh, qr):
    rows = ROWS * STEPS
    eye = hot_matrix(iota((ROPE, 128), 0) == iota((ROPE, 128), 1))
    side = jnp.zeros((ROPE, 128), BF16)
    below = jnp.zeros((ROPE, LATENT), BF16)
    for h in range(HEADS):
        base = (h // 2) * 384 + (h % 2) * 128
        window = dq_ref[:, base : base + 256]
        weight = wkt[h * NOPE : (h + 1) * NOPE, :]
        lat = [below, weight, below] if h % 2 else [weight, below, below]
        rot = [side, side, side, eye] if h % 2 else [side, side, eye, side]
        qh[h * rows : (h + 1) * rows, :LATENT] = mm(window, jnp.concatenate(lat, axis=0)).astype(BF16)
        qh[h * rows : (h + 1) * rows, LATENT:] = mm(window, jnp.concatenate(rot, axis=0)).astype(BF16)
    count = rows * HEADS
    order = hot_matrix(to_row_major(iota((count, count), 0)) == iota((count, count), 1))
    qr[...] = mm(order, qh[...]).astype(BF16)


def scores_of(queries, lat, rope):
    return mm(queries[:, :LATENT], lat) + mm(queries[:, LATENT:WIDTH], rope)


def decode_resident(qr, ct_ref, fresh_ref, rlen_ref, sr, ar, lo):
    per = STEPS * HEADS
    for r in range(ROWS):
        rows = slice(r * per, (r + 1) * per)
        sr[rows, :] = scores_of(
            qr[rows, :], ct_ref[r * WIDTH : r * WIDTH + LATENT, :], ct_ref[r * WIDTH + LATENT : (r + 1) * WIDTH, :]
        )
    count = ROWS * per
    row_of = iota((count, BLOCK), 0) // per
    filled = spread(row_of, [rlen_ref[r] for r in range(ROWS)], 0)
    s = jnp.where(iota((count, BLOCK), 1) < filled, sr[...], -BIG) * FACTOR
    fs = mm_nt(qr[:, :LATENT], fresh_ref[:, :LATENT]) + mm_nt(qr[:, LATENT:WIDTH], fresh_ref[:, LATENT:])
    place, col = iota(fs.shape, 0), iota(fs.shape, 1)
    open_ = (place // per == col // STEPS) & (col % STEPS <= (place // HEADS) % STEPS)
    fs = jnp.where(open_, fs, -BIG) * FACTOR
    best = jnp.maximum(jnp.max(s, axis=1, keepdims=True), jnp.max(fs, axis=1, keepdims=True))
    w = jnp.exp2(s - best)
    fw = jnp.exp2(fs - best)
    total = jnp.sum(w, axis=1, keepdims=True) + jnp.sum(fw, axis=1, keepdims=True)
    sr[...] = w
    for r in range(ROWS):
        rows = slice(r * per, (r + 1) * per)
        ar[rows, :] = mm_nt(sr[rows, :].astype(BF16), ct_ref[r * WIDTH : r * WIDTH + LATENT, :])
    lo[...] = ((ar[...] + mm(fw.astype(BF16), fresh_ref[:, :LATENT])) / total).astype(BF16)


def slot_table(me, lens_ref, place_ref, starts):
    rank = jnp.int32(0)
    row = [jnp.int32(-1)] * 2
    first = [jnp.int32(0)] * 2
    length = [jnp.int32(0)] * 2
    for j in range(NREQ):
        there = place_ref[j] // ROWS == me
        for k in range(2):
            hit = there & (rank == k)
            row[k] = jnp.where(hit, place_ref[j] % ROWS, row[k])
            first[k] = jnp.where(hit, starts[j], first[k])
            length[k] = jnp.where(hit, lens_ref[j], length[k])
        rank = rank + there.astype(jnp.int32)
    return row, first, length


def slot_queries(table, qr, qs2):
    per = STEPS * HEADS
    shape = (2 * per, ROWS * per)
    place = iota(shape, 0)
    row = spread(place // per, table[0], -1)
    pick = hot_matrix((row >= 0) & (iota(shape, 1) == row * per + place % per))
    qs2[...] = mm(pick, qr[...]).astype(BF16)


def slot_scores(block, g_ref, qs2, ss):
    ss[block] = scores_of(qs2[...], latent_rows(g_ref, block, 0, LATENT), latent_rows(g_ref, block, LATENT, ROPE))


def decode_slots(table, g_ref, qs2, ss, fresh_ref, lo_ref, out_rows):
    per = STEPS * HEADS
    row, first, length = table
    lines = 2 * per
    slot = iota((lines, BLOCK), 0) // per
    low = spread(slot, first, 0)
    high = low + spread(slot, length, 0)
    fs = mm_nt(qs2[:, :LATENT], fresh_ref[:, :LATENT]) + mm_nt(qs2[:, LATENT:WIDTH], fresh_ref[:, LATENT:])
    place, col = iota(fs.shape, 0), iota(fs.shape, 1)
    open_ = (spread(place // per, row, -1) == col // STEPS) & (col % STEPS <= (place // HEADS) % STEPS)
    fs = jnp.where(open_, fs, -BIG) * FACTOR
    best = jnp.max(fs, axis=1, keepdims=True)
    peak = jnp.full((lines, BLOCK), -BIG, F32)
    for b in range(N_CTX):
        pos = b * BLOCK + iota((lines, BLOCK), 1)
        s = jnp.where((pos >= low) & (pos < high), ss[b] * FACTOR, -BIG)
        ss[b] = s
        peak = jnp.maximum(peak, s)
    best = jnp.maximum(best, jnp.max(peak, axis=1, keepdims=True))
    fw = jnp.exp2(fs - best)
    mass = jnp.zeros((lines, BLOCK), F32)
    total = mm(fw.astype(BF16), fresh_ref[:, :LATENT])
    for b in range(N_CTX):
        w = jnp.exp2(ss[b] - best)
        mass = mass + w
        total = total + mm_nt(w.astype(BF16), latent_rows(g_ref, b, 0, LATENT))
    weight = jnp.sum(mass, axis=1, keepdims=True) + jnp.sum(fw, axis=1, keepdims=True)
    slot_out = (total / weight).astype(BF16)
    shape = (ROWS * per, lines)
    back = iota(shape, 1)
    back_row = spread(back // per, row, -1)
    route = hot_matrix((back_row >= 0) & (iota(shape, 0) == back_row * per + back % per))
    spot = iota((ROWS * per, LATENT), 0) // per
    replaced = (spot == row[0]) | (spot == row[1])
    out_rows[...] = jnp.where(replaced, mm(route, slot_out), lo_ref[...].astype(F32)).astype(BF16)


def head_values(rows_ref, wv_ref, x_ref):
    rows = ROWS * STEPS
    count = rows * HEADS
    order = hot_matrix(iota((count, count), 0) == to_row_major(iota((count, count), 1)))
    lat = mm(order, rows_ref[...]).astype(BF16)
    for h in range(HEADS):
        head = slice(h * NOPE, (h + 1) * NOPE)
        x_ref[:, head] = mm(lat[h * rows : (h + 1) * rows, :], wv_ref[:, head]).astype(BF16)


def attention_kernel(
    me_of,
    lens_ref,
    place_ref,
    rlen_ref,
    q_ref,
    g_ref,
    wk_ref,
    wv_ref,
    ct_ref,
    dq_ref,
    fresh_ref,
    out_ref,
    x_ref,
    wkt,
    wvt,
    qs,
    kt,
    vt,
    best,
    acc,
    qh,
    qr,
    sr,
    ar,
    lo,
    qs2,
    ss,
    lo2,
):
    me = me_of()
    starts, ends = request_table(lens_ref)
    table = slot_table(me, lens_ref, place_ref, starts)
    prepare_weights(wk_ref, wv_ref, wkt, wvt)
    decode_queries(dq_ref, wkt, qh, qr)
    slot_queries(table, qr, qs2)
    decode_resident(qr, ct_ref, fresh_ref, rlen_ref, sr, ar, lo)
    prepare_queries(me, q_ref, starts, ends, qs)
    step = functools.partial(
        attend_pair,
        me=me,
        g_ref=g_ref,
        starts=starts,
        ends=ends,
        wkt=wkt,
        wvt=wvt,
        qs=qs,
        kt=kt,
        vt=vt,
        best=best,
        acc=acc,
    )
    own = me // 2
    step(own, True)

    @pl.loop(jnp.maximum(own - 5, 0), own)
    def _(pair):
        step(pair, False)

    finish_prefill(acc, out_ref)

    @pl.loop(0, N_CTX)
    def _(b):
        slot_scores(b, g_ref, qs2, ss)

    decode_slots(table, g_ref, qs2, ss, fresh_ref, lo, lo2)
    head_values(lo2, wv_ref, x_ref)


def attention(me_of, lens, place, rlen, q, g, wk, wv, ct, dq, fresh):
    smem = pl.BlockSpec(memory_space=pltpu.SMEM)
    vmem = pl.BlockSpec(memory_space=pltpu.VMEM)
    lines = ROWS * STEPS * HEADS
    two = 2 * STEPS * HEADS
    return pl.pallas_call(
        functools.partial(attention_kernel, me_of),
        out_shape=(
            jax.ShapeDtypeStruct((BLOCK, HEADS * NOPE), BF16),
            jax.ShapeDtypeStruct((ROWS * STEPS, HEADS * NOPE), BF16),
        ),
        in_specs=[smem] * 3 + [vmem] * 7,
        out_specs=(vmem, vmem),
        scratch_shapes=[
            pltpu.VMEM((HEADS * NOPE, LATENT), BF16),
            pltpu.VMEM((HEADS * NOPE, LATENT), BF16),
            pltpu.VMEM((HEADS, BLOCK, 256), BF16),
            pltpu.VMEM((HEADS * NOPE, 2 * BLOCK), BF16),
            pltpu.VMEM((HEADS * NOPE, 2 * BLOCK), BF16),
            pltpu.VMEM((HEADS, BLOCK, 128), F32),
            pltpu.VMEM((HEADS, BLOCK, 256), F32),
            pltpu.VMEM((lines, 640), BF16),
            pltpu.VMEM((lines, 640), BF16),
            pltpu.VMEM((lines, BLOCK), F32),
            pltpu.VMEM((lines, LATENT), F32),
            pltpu.VMEM((lines, LATENT), BF16),
            pltpu.VMEM((two, 640), BF16),
            pltpu.VMEM((N_CTX, two, BLOCK), F32),
            pltpu.VMEM((lines, LATENT), BF16),
        ],
        compiler_params=pltpu.CompilerParams(vmem_limit_bytes=60 * MIB),
        name="attention",
    )(lens, place, rlen, q, g, wk, wv, ct, dq, fresh)


CHUNKS = (2048, 2048, 2048, 1024)


def project_kernel(x_ref, w_ref, out_ref, w_buf, send, recv, w_sem, send_sem, recv_sem):
    ctx, tp = chip_parts()
    loads = []
    first = 0
    for c, width in enumerate(CHUNKS):
        cols = slice(first, first + width)
        loads.append(pltpu.make_async_copy(w_ref.at[:, cols], w_buf.at[:, cols], w_sem.at[c]))
        first += width
    for load in loads:
        load.start()
    barrier = pltpu.get_barrier_semaphore()
    for d in range(1, N_TP):
        pl.semaphore_signal(barrier, inc=1, device_id=(ctx, lax.rem(tp + d, N_TP)), device_id_type=MESH)
    pl.semaphore_wait(barrier, N_TP - 1)
    copies = []
    first = 0
    for c, width in enumerate(CHUNKS):
        quarter = width // 4
        q0 = first // 4
        loads[c].wait()
        part = mm(x_ref[...], w_buf[:, first : first + width])
        for p in range(N_TP):
            rows = part[4 * p : 4 * p + 4, :]
            piece = jnp.concatenate([rows[:, k * quarter : (k + 1) * quarter] for k in range(4)], axis=0)
            send[p, :, q0 : q0 + quarter] = piece.astype(BF16)
        for d in range(1, N_TP):
            peer = lax.rem(tp + d, N_TP)
            copy = pltpu.make_async_remote_copy(
                src_ref=send.at[peer, :, q0 : q0 + quarter],
                dst_ref=recv.at[d, :, q0 : q0 + quarter],
                send_sem=send_sem.at[c, d],
                recv_sem=recv_sem.at[c, d],
                device_id=(ctx, peer),
                device_id_type=MESH,
            )
            copy.start()
            copies.append((c, d, copy))
        first += width
    first = 0
    for c, width in enumerate(CHUNKS):
        quarter = width // 4
        q0 = first // 4
        total = send[tp, :, q0 : q0 + quarter].astype(F32)
        for c2, d, copy in copies:
            if c2 == c:
                copy.wait_recv()
                total = total + recv[d, :, q0 : q0 + quarter].astype(F32)
        for k in range(4):
            out_ref[:, first + k * quarter : first + (k + 1) * quarter] = total[4 * k : 4 * k + 4, :].astype(BF16)
        first += width
    for _, _, copy in copies:
        copy.wait_send()


def project(x, w):
    width = w.shape[1]
    return pl.pallas_call(
        project_kernel,
        out_shape=jax.ShapeDtypeStruct((4, width), BF16),
        in_specs=[pl.BlockSpec(memory_space=pltpu.VMEM), pl.BlockSpec(memory_space=pl.ANY)],
        out_specs=pl.BlockSpec(memory_space=pltpu.VMEM),
        scratch_shapes=[
            pltpu.VMEM(w.shape, BF16),
            pltpu.VMEM((N_TP, 16, width // 4), BF16),
            pltpu.VMEM((N_TP, 16, width // 4), BF16),
            pltpu.SemaphoreType.DMA((len(CHUNKS),)),
            pltpu.SemaphoreType.DMA((len(CHUNKS), N_TP)),
            pltpu.SemaphoreType.DMA((len(CHUNKS), N_TP)),
        ],
        compiler_params=pltpu.CompilerParams(collective_id=1, has_side_effects=True, vmem_limit_bytes=60 * MIB),
        name="project",
    )(x, w)


def on_device(
    prefill_query,
    span_latent,
    prompt_lengths,
    key_weight,
    value_weight,
    placement,
    resident_cache,
    resident_lengths,
    decode_query,
    decode_latent,
    out_weight,
):
    latents = gather(span_latent.T)
    cache_t = jnp.swapaxes(resident_cache, 1, 2).reshape(ROWS * WIDTH, BLOCK)
    prefill_out, mixed = attention(
        lambda: lax.axis_index("ctx"),
        prompt_lengths,
        placement,
        resident_lengths,
        prefill_query,
        latents,
        key_weight,
        value_weight,
        cache_t,
        decode_query.reshape(ROWS * STEPS, -1),
        decode_latent.reshape(ROWS * STEPS, -1),
    )
    decode_out = project(mixed, out_weight).reshape(2, STEPS, -1)
    return (prefill_out, decode_out)


def solution(mesh):
    placed = (
        P("ctx", "tp"),
        P("ctx", None),
        P(),
        P(None, "tp"),
        P(None, "tp"),
        P(),
        P("ctx", None, None),
        P("ctx"),
        P("ctx", None, "tp"),
        P("ctx", None, None),
        P("tp", None),
    )
    return jax.shard_map(
        on_device,
        mesh=mesh,
        in_specs=placed,
        out_specs=(P("ctx", "tp"), P(("ctx", "tp"), None, None)),
        check_vma=False,
    )
```

time: 217 us -> 109 us (0.50)
  the two profiles are of different devices: /device:TPU:1 before, /device:TPU:97 now
where the time goes in v1:
time: 109 us; the launch traced here: 108 us
  Pallas kernels  103 us (94%)
  local copies, waits for them, and re-layouts  4.49 us (4%)
    pallas_call x1, Pallas kernels, gather(): pl.pallas_call(gather_kernel, out_shape=jax.ShapeDtypeStruct((N_CTX * WID...  59.2 us
    pallas_call x1, Pallas kernels, attention(): pl.pallas_call(functools.partial(attention_kernel, me_of), out_shape=(jax...  29.6 us
    pallas_call x1, Pallas kernels, project(): pl.pallas_call(project_kernel, out_shape=jax.ShapeDtypeStruct((4, width),...  14.5 us

profile of v1, /device:TPU:97, one launch (start us, length us, event | category | flops | bytes accessed | tf_op | source)
XLA Modules:
  0.0 108.4 jit_solution(1090375517906587900)
XLA Ops:
  0.6 1.4 %reshape.18.fresh_ref = bf16[32,576]{1,0:T(8,128)(2,1)} reshape(bf16[16,2,576]{2,1,0:T(2,128)(2,1)} %param.20) | data formatting | bytes 73728 | tf_op jit(solution)/shard_map/reshape | solution.py:519
  2.1 1.6 %reshape.17.dq_ref = bf16[32,1536]{1,0:T(8,128)(2,1)} reshape(bf16[16,2,1536]{2,1,0:T(2,128)(2,1)} %param.19) | data formatting | bytes 196608 | tf_op jit(solution)/shard_map/reshape | solution.py:518
  3.6 59.2 %gather.1.g_ref = bf16[9216,256]{1,0:T(8,128)(2,1)} custom-call(bf16[576,256]{1,0:T(8,128)(2,1)} %bitcast.5), custom_call_target="tpu_custom_call" | custom-call | tf_op jit(solution)/shard_map/gather/pallas_call | solution.py:98
  62.9 29.6 %attention.1 = (bf16[256,1024]{1,0:T(8,128)(2,1)}, bf16[32,1024]{1,0:T(8,128)(2,1)}) custom-call(s32[8]{0:T(128)} %lens_ref.1, s32[8]{0:T(128)} %place_ref.1, s32[16]{0:T(128)} %rlen_ref.1, bf16[256,1536]{1,0:T(8,128)(2,1)} %q_ref.1, bf16[9216,256]{1,0:T(8,128)(2,1)} %gather.1.g_ref, bf16[512,1024]{1,0:T(8,128)(2,1)} %wk_ref.1, bf16[512,1024]{1,0:T(8,128)(2,1)} %wv_ref.1, ...), custom_call_target="tpu_custom_call" | custom-call | tf_op jit(solution)/shard_map/attention/pallas_call | solution.py:386
  92.5 14.5 %project.1 = bf16[4,7168]{1,0:T(4,128)(2,1)} custom-call(bf16[32,1024]{1,0:T(8,128)(2,1)} %get-tuple-element.5.x_ref, bf16[1024,7168]{1,0:T(8,128)(2,1)} %w_ref.1), custom_call_target="tpu_custom_call" | custom-call | tf_op jit(solution)/shard_map/project/pallas_call | solution.py:475
  106.9 1.5 %reshape.19 = bf16[2,2,7168]{2,1,0:T(2,128)(2,1)} reshape(bf16[4,7168]{1,0:T(4,128)(2,1)} %project.1) | data formatting | bytes 114688 | tf_op jit(solution)/shard_map/reshape | solution.py:521

commit v2 on v1

--- a/solution.py
+++ b/solution.py
@@ -25,6 +25,10 @@
 F32 = jnp.float32
 BF16 = jnp.bfloat16
 MIB = 1 << 20
+HALF = WIDTH // 2
+N_Z = 4
+N_STATION = 7
+CHUNKS = (2048, 2048, 2048, 1024)
 
 
 def mm(left, right):
@@ -53,61 +57,6 @@
     for j, value in enumerate(values):
         out = jnp.where(index == j, value, out)
     return out
-
-
-def chip_parts():
-    ctx = lax.axis_index("ctx")
-    tp = lax.axis_index("tp")
-    return ctx, tp
-
-
-def gather_kernel(own_ref, all_ref, send_sem, recv_sem, copy_sem):
-    ctx, tp = chip_parts()
-    barrier = pltpu.get_barrier_semaphore()
-    for d in range(1, N_CTX):
-        peer = lax.rem(ctx + d, N_CTX)
-        pl.semaphore_signal(barrier, inc=1, device_id=(peer, tp), device_id_type=MESH)
-    pl.semaphore_wait(barrier, N_CTX - 1)
-    mine = all_ref.at[pl.ds(pl.multiple_of(ctx * WIDTH, 64), WIDTH)]
-    local = pltpu.make_async_copy(own_ref, mine, copy_sem)
-    local.start()
-
-    def copy_to(d):
-        return pltpu.make_async_remote_copy(
-            src_ref=own_ref,
-            dst_ref=mine,
-            send_sem=send_sem.at[d],
-            recv_sem=recv_sem.at[d],
-            device_id=(lax.rem(ctx + d, N_CTX), tp),
-            device_id_type=MESH,
-        )
-
-    copies = [copy_to(d) for d in range(1, N_CTX)]
-    for c in copies:
-        c.start()
-    local.wait()
-    for d in range(1, N_CTX):
-        source = lax.rem(ctx - d + N_CTX, N_CTX)
-        theirs = all_ref.at[pl.ds(pl.multiple_of(source * WIDTH, 64), WIDTH)]
-        pltpu.make_async_copy(own_ref, theirs, recv_sem.at[d]).wait()
-    for c in copies:
-        c.wait_send()
-
-
-def gather(latent_t):
-    return pl.pallas_call(
-        gather_kernel,
-        out_shape=jax.ShapeDtypeStruct((N_CTX * WIDTH, BLOCK), BF16),
-        in_specs=[pl.BlockSpec(memory_space=pltpu.VMEM)],
-        out_specs=pl.BlockSpec(memory_space=pltpu.VMEM),
-        scratch_shapes=[
-            pltpu.SemaphoreType.DMA((N_CTX,)),
-            pltpu.SemaphoreType.DMA((N_CTX,)),
-            pltpu.SemaphoreType.DMA,
-        ],
-        compiler_params=pltpu.CompilerParams(collective_id=0, has_side_effects=True, vmem_limit_bytes=60 * MIB),
-        name="gather",
-    )(latent_t)
 
 
 def prepare_weights(wk_ref, wv_ref, wkt, wvt):
@@ -309,11 +258,56 @@
         x_ref[:, head] = mm(lat[h * rows : (h + 1) * rows, :], wv_ref[:, head]).astype(BF16)
 
 
-def attention_kernel(
-    me_of,
+def z_step(v):
+    zz = v // 2
+    return (zz * 3) % 5 - (zz // 3) * 2
+
+
+class Place:
+    def __init__(self):
+        self.ctx = lax.axis_index("ctx")
+        self.tp = lax.axis_index("tp")
+        self.core = self.ctx % 2
+        self.z = self.ctx // 4
+        self.x_lo = (self.ctx // 2) % 2
+        self.x = (self.tp // 4) * 2 + self.x_lo
+        self.y = self.tp % 4
+
+    def at(self, dz, dx):
+        z = (self.z + dz + N_Z) % N_Z
+        x = (self.x + dx + 4) % 4
+        return ((z * 2 + x % 2) * 2 + self.core, (x // 2) * 4 + self.y)
+
+    def sibling(self):
+        return (self.ctx + 1 - 2 * self.core, self.tp)
+
+    def station_pair(self, station):
+        v = station + 1
+        return ((self.z + z_step(v) + N_Z) % N_Z) * 2 + (self.x_lo + v) % 2
+
+
+def half_rows(g_ref, block, half):
+    return g_ref.at[pl.ds(pl.multiple_of(block * WIDTH + half * HALF, 32), HALF)]
+
+
+def block_rows(g_ref, block):
+    return g_ref.at[pl.ds(pl.multiple_of(block * WIDTH, 64), WIDTH)]
+
+
+def mega_kernel(
     lens_ref,
     place_ref,
     rlen_ref,
+    q_hbm,
+    own_hbm,
+    wk_hbm,
+    wv_hbm,
+    ct_hbm,
+    dq_hbm,
+    fresh_hbm,
+    w_hbm,
+    out_hbm,
+    dec_ref,
     q_ref,
     g_ref,
     wk_ref,
@@ -321,6 +315,7 @@
     ct_ref,
     dq_ref,
     fresh_ref,
+    w_ref,
     out_ref,
     x_ref,
     wkt,
@@ -338,15 +333,129 @@
     qs2,
     ss,
     lo2,
+    send,
+    recv,
+    load_sem,
+    w_sem,
+    link_send,
+    link_recv,
+    core_send,
+    core_recv,
+    sum_send,
+    sum_recv,
 ):
-    me = me_of()
+    at = Place()
+    me, tp = at.ctx, at.tp
+    barrier = pltpu.get_barrier_semaphore()
+    peers = [at.sibling()]
+    peers += [at.at(dz, dx) for dz in (-1, 1) for dx in (-1, 0, 1)] + [at.at(0, -1), at.at(0, 1)]
+    peers += [(me, (tp + d) % N_TP) for d in range(1, N_TP)]
+    for peer in peers:
+        pl.semaphore_signal(barrier, inc=1, device_id=peer, device_id_type=MESH)
+
+    pairs = [
+        (wk_hbm, wk_ref),
+        (wv_hbm, wv_ref),
+        (dq_hbm, dq_ref),
+        (fresh_hbm, fresh_ref),
+        (ct_hbm, ct_ref),
+        (q_hbm, q_ref),
+        (own_hbm, block_rows(g_ref, me)),
+    ]
+    loads = [pltpu.make_async_copy(src, dst, load_sem.at[i]) for i, (src, dst) in enumerate(pairs)]
+    for load in loads:
+        load.start()
+    pl.semaphore_wait(barrier, len(peers))
+
+    sent = []
+
+    def push(src, block, half, station, device):
+        copy = pltpu.make_async_remote_copy(
+            src_ref=src,
+            dst_ref=half_rows(g_ref, block, half),
+            send_sem=link_send.at[station, half],
+            recv_sem=link_recv.at[station, half],
+            device_id=device,
+            device_id_type=MESH,
+        )
+        copy.start()
+        sent.append(copy)
+
+    def own_half(half):
+        return own_hbm.at[half * HALF : (half + 1) * HALF]
+
+    own_to_core = pltpu.make_async_remote_copy(
+        src_ref=own_hbm,
+        dst_ref=block_rows(g_ref, me),
+        send_sem=core_send.at[N_STATION],
+        recv_sem=core_recv.at[N_STATION],
+        device_id=at.sibling(),
+        device_id_type=MESH,
+    )
+    own_to_core.start()
+    sent.append(own_to_core)
+    for dz, station in ((1, 1), (0, 0), (-1, 3)):
+        for half in range(2):
+            if dz:
+                push(own_half(half), me, half, station, at.at(dz, 0))
+            push(own_half(half), me, half, station + (1 if dz else 0), at.at(dz, 2 * half - 1))
+
+    def landed(station, half):
+        block = 2 * at.station_pair(station) + at.core
+        pltpu.make_async_copy(own_half(half), half_rows(g_ref, block, half), link_recv.at[station, half]).wait()
+
+    def relay(station):
+        half = 0 if station < 3 else 1
+        block = 2 * at.station_pair(station) + at.core
+        push(half_rows(g_ref, block, half), block, half, 5 + (station + 1) % 2, at.at(1 if station < 3 else -1, 0))
+
+    def to_core(station):
+        block = 2 * at.station_pair(station) + at.core
+        copy = pltpu.make_async_remote_copy(
+            src_ref=block_rows(g_ref, block),
+            dst_ref=block_rows(g_ref, block),
+            send_sem=core_send.at[station],
+            recv_sem=core_recv.at[station],
+            device_id=at.sibling(),
+            device_id_type=MESH,
+        )
+        copy.start()
+        sent.append(copy)
+
+    def from_core(station, pair):
+        block = 2 * pair + 1 - at.core
+        pltpu.make_async_copy(own_hbm, block_rows(g_ref, block), core_recv.at[station]).wait()
+
     starts, ends = request_table(lens_ref)
     table = slot_table(me, lens_ref, place_ref, starts)
+    loads[0].wait()
+    loads[1].wait()
     prepare_weights(wk_ref, wv_ref, wkt, wvt)
+    loads[2].wait()
+    loads[3].wait()
     decode_queries(dq_ref, wkt, qh, qr)
     slot_queries(table, qr, qs2)
+    loads[4].wait()
+    w_loads = []
+    first = 0
+    for c, width in enumerate(CHUNKS):
+        cols = slice(first, first + width)
+        w_loads.append(pltpu.make_async_copy(w_hbm.at[:, cols], w_ref.at[:, cols], w_sem.at[c]))
+        w_loads[-1].start()
+        first += width
     decode_resident(qr, ct_ref, fresh_ref, rlen_ref, sr, ar, lo)
+    loads[5].wait()
     prepare_queries(me, q_ref, starts, ends, qs)
+
+    for station in (1, 3):
+        for half in range(2):
+            landed(station, half)
+        relay(station)
+    for half in range(2):
+        landed(0, half)
+    for station in (0, 1, 3):
+        to_core(station)
+
     step = functools.partial(
         attend_pair,
         me=me,
@@ -362,36 +471,128 @@
         acc=acc,
     )
     own = me // 2
+    loads[6].wait()
+    from_core(N_STATION, own)
     step(own, True)
 
-    @pl.loop(jnp.maximum(own - 5, 0), own)
-    def _(pair):
-        step(pair, False)
-
-    finish_prefill(acc, out_ref)
-
-    @pl.loop(0, N_CTX)
-    def _(b):
+    for station in (2, 4):
+        for half in range(2):
+            landed(station, half)
+        relay(station)
+        to_core(station)
+
+    def project():
+        copies = []
+        first = 0
+        for c, width in enumerate(CHUNKS):
+            quarter = width // 4
+            q0 = first // 4
+            w_loads[c].wait()
+            part = mm(x_ref[...], w_ref[:, first : first + width])
+            for p in range(N_TP):
+                rows = part[4 * p : 4 * p + 4, :]
+                piece = jnp.concatenate([rows[:, k * quarter : (k + 1) * quarter] for k in range(4)], axis=0)
+                send[p, :, q0 : q0 + quarter] = piece.astype(BF16)
+            for d in range(1, N_TP):
+                peer = (tp + d) % N_TP
+                copy = pltpu.make_async_remote_copy(
+                    src_ref=send.at[peer, :, q0 : q0 + quarter],
+                    dst_ref=recv.at[d, :, q0 : q0 + quarter],
+                    send_sem=sum_send.at[c, d],
+                    recv_sem=sum_recv.at[c, d],
+                    device_id=(me, peer),
+                    device_id_type=MESH,
+                )
+                copy.start()
+                copies.append((c, d, copy))
+            first += width
+        return copies
+
+    def near(station):
+        pair = at.station_pair(station)
+        from_core(station, pair)
+
+        @pl.when((pair < own) & (pair >= own - 5))
+        def _():
+            step(pair, False)
+
+    @pl.loop(0, 5)
+    def _(station):
+        near(station)
+
+    for station in (5, 6):
+        for half in range(2):
+            landed(station, half)
+        to_core(station)
+    for station in (5, 6):
+        from_core(station, at.station_pair(station))
+
+    for b in range(N_CTX):
         slot_scores(b, g_ref, qs2, ss)
-
     decode_slots(table, g_ref, qs2, ss, fresh_ref, lo, lo2)
     head_values(lo2, wv_ref, x_ref)
-
-
-def attention(me_of, lens, place, rlen, q, g, wk, wv, ct, dq, fresh):
+    sums = project()
+
+    @pl.loop(5, N_STATION)
+    def _(station):
+        pair = at.station_pair(station)
+
+        @pl.when((pair < own) & (pair >= own - 5))
+        def _():
+            step(pair, False)
+
+    finish_prefill(acc, out_ref)
+    store = pltpu.make_async_copy(out_ref, out_hbm, load_sem.at[len(pairs)])
+    store.start()
+
+    first = 0
+    for c, width in enumerate(CHUNKS):
+        quarter = width // 4
+        q0 = first // 4
+        total = send[tp, :, q0 : q0 + quarter].astype(F32)
+        for c2, d, copy in sums:
+            if c2 == c:
+                copy.wait_recv()
+                total = total + recv[d, :, q0 : q0 + quarter].astype(F32)
+        for k in range(4):
+            for row in range(2):
+                piece = total[4 * k + 2 * row : 4 * k + 2 * row + 2, :]
+                dec_ref[row, :, first + k * quarter : first + (k + 1) * quarter] = piece.astype(BF16)
+        first += width
+    for _, _, copy in sums:
+        copy.wait_send()
+    for copy in sent:
+        copy.wait_send()
+    store.wait()
+
+
+def mega(lens, place, rlen, q, own, wk, wv, ct, dq, fresh, w):
     smem = pl.BlockSpec(memory_space=pltpu.SMEM)
     vmem = pl.BlockSpec(memory_space=pltpu.VMEM)
+    far = pl.BlockSpec(memory_space=pl.ANY)
     lines = ROWS * STEPS * HEADS
     two = 2 * STEPS * HEADS
+    width = w.shape[1]
+    dma = pltpu.SemaphoreType.DMA
     return pl.pallas_call(
-        functools.partial(attention_kernel, me_of),
+        mega_kernel,
         out_shape=(
             jax.ShapeDtypeStruct((BLOCK, HEADS * NOPE), BF16),
-            jax.ShapeDtypeStruct((ROWS * STEPS, HEADS * NOPE), BF16),
+            jax.ShapeDtypeStruct((2, STEPS, width), BF16),
         ),
-        in_specs=[smem] * 3 + [vmem] * 7,
-        out_specs=(vmem, vmem),
+        in_specs=[smem] * 3 + [far] * 8,
+        out_specs=(far, vmem),
         scratch_shapes=[
+            pltpu.VMEM(q.shape, BF16),
+            pltpu.VMEM((N_CTX * WIDTH, BLOCK), BF16),
+            pltpu.VMEM(wk.shape, BF16),
+            pltpu.VMEM(wv.shape, BF16),
+            pltpu.VMEM(ct.shape, BF16),
+            pltpu.VMEM(dq.shape, BF16),
+            pltpu.VMEM(fresh.shape, BF16),
+            pltpu.VMEM(w.shape, BF16),
+            pltpu.VMEM((BLOCK, HEADS * NOPE), BF16),
+            pltpu.VMEM((ROWS * STEPS, HEADS * NOPE), BF16),
             pltpu.VMEM((HEADS * NOPE, LATENT), BF16),
             pltpu.VMEM((HEADS * NOPE, LATENT), BF16),
             pltpu.VMEM((HEADS, BLOCK, 256), BF16),
@@ -407,87 +608,20 @@
             pltpu.VMEM((two, 640), BF16),
             pltpu.VMEM((N_CTX, two, BLOCK), F32),
             pltpu.VMEM((lines, LATENT), BF16),
-        ],
-        compiler_params=pltpu.CompilerParams(vmem_limit_bytes=60 * MIB),
-        name="attention",
-    )(lens, place, rlen, q, g, wk, wv, ct, dq, fresh)
-
-
-CHUNKS = (2048, 2048, 2048, 1024)
-
-
-def project_kernel(x_ref, w_ref, out_ref, w_buf, send, recv, w_sem, send_sem, recv_sem):
-    ctx, tp = chip_parts()
-    loads = []
-    first = 0
-    for c, width in enumerate(CHUNKS):
-        cols = slice(first, first + width)
-        loads.append(pltpu.make_async_copy(w_ref.at[:, cols], w_buf.at[:, cols], w_sem.at[c]))
-        first += width
-    for load in loads:
-        load.start()
-    barrier = pltpu.get_barrier_semaphore()
-    for d in range(1, N_TP):
-        pl.semaphore_signal(barrier, inc=1, device_id=(ctx, lax.rem(tp + d, N_TP)), device_id_type=MESH)
-    pl.semaphore_wait(barrier, N_TP - 1)
-    copies = []
-    first = 0
-    for c, width in enumerate(CHUNKS):
-        quarter = width // 4
-        q0 = first // 4
-        loads[c].wait()
-        part = mm(x_ref[...], w_buf[:, first : first + width])
-        for p in range(N_TP):
-            rows = part[4 * p : 4 * p + 4, :]
-            piece = jnp.concatenate([rows[:, k * quarter : (k + 1) * quarter] for k in range(4)], axis=0)
-            send[p, :, q0 : q0 + quarter] = piece.astype(BF16)
-        for d in range(1, N_TP):
-            peer = lax.rem(tp + d, N_TP)
-            copy = pltpu.make_async_remote_copy(
-                src_ref=send.at[peer, :, q0 : q0 + quarter],
-                dst_ref=recv.at[d, :, q0 : q0 + quarter],
-                send_sem=send_sem.at[c, d],
-                recv_sem=recv_sem.at[c, d],
-                device_id=(ctx, peer),
-                device_id_type=MESH,
-            )
-            copy.start()
-            copies.append((c, d, copy))
-        first += width
-    first = 0
-    for c, width in enumerate(CHUNKS):
-        quarter = width // 4
-        q0 = first // 4
-        total = send[tp, :, q0 : q0 + quarter].astype(F32)
-        for c2, d, copy in copies:
-            if c2 == c:
-                copy.wait_recv()
-                total = total + recv[d, :, q0 : q0 + quarter].astype(F32)
-        for k in range(4):
-            out_ref[:, first + k * quarter : first + (k + 1) * quarter] = total[4 * k : 4 * k + 4, :].astype(BF16)
-        first += width
-    for _, _, copy in copies:
-        copy.wait_send()
-
-
-def project(x, w):
-    width = w.shape[1]
-    return pl.pallas_call(
-        project_kernel,
-        out_shape=jax.ShapeDtypeStruct((4, width), BF16),
-        in_specs=[pl.BlockSpec(memory_space=pltpu.VMEM), pl.BlockSpec(memory_space=pl.ANY)],
-        out_specs=pl.BlockSpec(memory_space=pltpu.VMEM),
-        scratch_shapes=[
-            pltpu.VMEM(w.shape, BF16),
             pltpu.VMEM((N_TP, 16, width // 4), BF16),
             pltpu.VMEM((N_TP, 16, width // 4), BF16),
-            pltpu.SemaphoreType.DMA((len(CHUNKS),)),
-            pltpu.SemaphoreType.DMA((len(CHUNKS), N_TP)),
-            pltpu.SemaphoreType.DMA((len(CHUNKS), N_TP)),
+            dma((8,)),
+            dma((len(CHUNKS),)),
+            dma((N_STATION, 2)),
+            dma((N_STATION, 2)),
+            dma((N_STATION + 1,)),
+            dma((N_STATION + 1,)),
+            dma((len(CHUNKS), N_TP)),
+            dma((len(CHUNKS), N_TP)),
         ],
-        compiler_params=pltpu.CompilerParams(collective_id=1, has_side_effects=True, vmem_limit_bytes=60 * MIB),
-        name="project",
-    )(x, w)
+        compiler_params=pltpu.CompilerParams(collective_id=0, has_side_effects=True, vmem_limit_bytes=60 * MIB),
+        name="latent_attention",
+    )(lens, place, rlen, q, own, wk, wv, ct, dq, fresh, w)
 
 
 def on_device(
@@ -503,23 +637,20 @@
     decode_latent,
     out_weight,
 ):
-    latents = gather(span_latent.T)
     cache_t = jnp.swapaxes(resident_cache, 1, 2).reshape(ROWS * WIDTH, BLOCK)
-    prefill_out, mixed = attention(
-        lambda: lax.axis_index("ctx"),
+    return mega(
         prompt_lengths,
         placement,
         resident_lengths,
         prefill_query,
-        latents,
+        span_latent.T,
         key_weight,
         value_weight,
         cache_t,
         decode_query.reshape(ROWS * STEPS, -1),
         decode_latent.reshape(ROWS * STEPS, -1),
+        out_weight,
     )
-    decode_out = project(mixed, out_weight).reshape(2, STEPS, -1)
-    return (prefill_out, decode_out)
 
 
 def solution(mesh):

time: 109 us -> 55.7 us (0.51)
  Pallas kernels: 103 us -> 48 us
  local copies, waits for them, and re-layouts: 4.49 us -> 6.36 us
    pallas_call x3 -> x1, Pallas kernels: 103 us -> 48 us  [mega(): pl.pallas_call(mega_kernel, out_shape=(jax.ShapeDtypeStruct((BLOCK, HEADS...]
    unnamed x0 -> x2, local copies, waits for them, and re-layouts: none -> 3.35 us
    reshape x1 -> x0, local copies, waits for them, and re-layouts: 1.47 us -> none  [on_device(): decode_out = project(mixed, out_weight).reshape(2, STEPS, -1)]
where the time goes in v2:
time: 55.7 us; the launch traced here: 55 us
  Pallas kernels  48 us (86%)
  local copies, waits for them, and re-layouts  6.36 us (11%)
  between operations  0.64 us (1%)
    pallas_call x1, Pallas kernels, mega(): pl.pallas_call(mega_kernel, out_shape=(jax.ShapeDtypeStruct((BLOCK, HEADS...  48 us
    unnamed x2, local copies, waits for them, and re-layouts  3.35 us
    reshape x1, local copies, waits for them, and re-layouts, on_device(): decode_query.reshape(ROWS * STEPS, -1)  1.57 us
    reshape x1, local copies, waits for them, and re-layouts, on_device(): decode_latent.reshape(ROWS * STEPS, -1)  1.44 us

profile of v2, /device:TPU:97, one launch (start us, length us, event | category | flops | bytes accessed | tf_op | source)
XLA Modules:
  0.0 55.0 jit_solution(15927252072083408036)
XLA Ops:
  0.6 1.4 %reshape.15.fresh_hbm = bf16[32,576]{1,0:T(8,128)(2,1)} reshape(bf16[16,2,576]{2,1,0:T(2,128)(2,1)} %param.20) | data formatting | bytes 73728 | tf_op jit(solution)/shard_map/reshape | solution.py:651
  2.1 1.6 %reshape.14.dq_hbm = bf16[32,1536]{1,0:T(8,128)(2,1)} reshape(bf16[16,2,1536]{2,1,0:T(2,128)(2,1)} %param.19) | data formatting | bytes 196608 | tf_op jit(solution)/shard_map/reshape | solution.py:650
  3.6 48.0 %latent_attention.1 = (bf16[256,1024]{1,0:T(8,128)(2,1)}, bf16[2,2,7168]{2,1,0:T(2,128)(2,1)}) custom-call(s32[8]{0:T(128)} %lens_ref.1, s32[8]{0:T(128)} %place_ref.1, s32[16]{0:T(128)} %rlen_ref.1, bf16[256,1536]{1,0:T(8,128)(2,1)} %q_hbm.1, bf16[576,256]{1,0:T(8,128)(2,1)} %bitcast.5, bf16[512,1024]{1,0:T(8,128)(2,1)} %wk_hbm.1, ...), custom_call_target="tpu_custom_call" | custom-call | tf_op jit(solution)/shard_map/latent_attention/pallas_call | solution.py:577
  51.7 1.9 %copy.15 = bf16[256,1024]{1,0:T(8,128)(2,1)} copy(bf16[256,1024]{1,0:T(8,128)(2,1)} %get-tuple-element.4) | data formatting | bytes 1048576
  53.5 1.5 %copy.16 = bf16[2,2,7168]{2,1,0:T(2,128)(2,1)} copy(bf16[2,2,7168]{2,1,0:T(2,128)(2,1)} %get-tuple-element.5) | data formatting | bytes 114688

commit v3 on v2

--- a/solution.py
+++ b/solution.py
@@ -26,8 +26,10 @@
 BF16 = jnp.bfloat16
 MIB = 1 << 20
 HALF = WIDTH // 2
+QUARTER = WIDTH // 4
 N_Z = 4
 N_STATION = 7
+FAR = (5, 6, 4)
 CHUNKS = (2048, 2048, 2048, 1024)
 
 
@@ -134,6 +136,12 @@
     return condition.astype(F32).astype(BF16)
 
 
+def pack_rows(rows_ref, wide_ref, flat_ref):
+    for r in range(ROWS):
+        wide_ref[r * STEPS : (r + 1) * STEPS, :] = rows_ref[r].astype(F32)
+    flat_ref[...] = wide_ref[...].astype(BF16)
+
+
 def decode_queries(dq_ref, wkt, qh, qr):
     rows = ROWS * STEPS
     eye = hot_matrix(iota((ROPE, 128), 0) == iota((ROPE, 128), 1))
@@ -273,10 +281,11 @@
         self.x = (self.tp // 4) * 2 + self.x_lo
         self.y = self.tp % 4
 
-    def at(self, dz, dx):
+    def at(self, dz, dx, dy=0):
         z = (self.z + dz + N_Z) % N_Z
         x = (self.x + dx + 4) % 4
-        return ((z * 2 + x % 2) * 2 + self.core, (x // 2) * 4 + self.y)
+        y = (self.y + dy + 4) % 4
+        return ((z * 2 + x % 2) * 2 + self.core, (x // 2) * 4 + y)
 
     def sibling(self):
         return (self.ctx + 1 - 2 * self.core, self.tp)
@@ -288,6 +297,10 @@
 
 def half_rows(g_ref, block, half):
     return g_ref.at[pl.ds(pl.multiple_of(block * WIDTH + half * HALF, 32), HALF)]
+
+
+def quarter_rows(g_ref, block, quarter):
+    return g_ref.at[pl.ds(pl.multiple_of(block * WIDTH + quarter * QUARTER, 16), QUARTER)]
 
 
 def block_rows(g_ref, block):
@@ -315,6 +328,10 @@
     ct_ref,
     dq_ref,
     fresh_ref,
+    dq3,
+    fresh3,
+    dq32,
+    fresh32,
     w_ref,
     out_ref,
     x_ref,
@@ -339,6 +356,8 @@
     w_sem,
     link_send,
     link_recv,
+    far_send,
+    far_recv,
     core_send,
     core_recv,
     sum_send,
@@ -348,7 +367,9 @@
     me, tp = at.ctx, at.tp
     barrier = pltpu.get_barrier_semaphore()
     peers = [at.sibling()]
-    peers += [at.at(dz, dx) for dz in (-1, 1) for dx in (-1, 0, 1)] + [at.at(0, -1), at.at(0, 1)]
+    aside = 1 - 2 * (at.y % 2)
+    peers += [at.at(1, 0), at.at(-1, 0), at.at(2, 0), at.at(0, -1), at.at(0, 1)]
+    peers += [at.at(2, 1), at.at(2, -1), at.at(1, 1), at.at(1, -1), at.at(-1, 1), at.at(-1, -1)]
     peers += [(me, (tp + d) % N_TP) for d in range(1, N_TP)]
     for peer in peers:
         pl.semaphore_signal(barrier, inc=1, device_id=peer, device_id_type=MESH)
@@ -356,8 +377,8 @@
     pairs = [
         (wk_hbm, wk_ref),
         (wv_hbm, wv_ref),
-        (dq_hbm, dq_ref),
-        (fresh_hbm, fresh_ref),
+        (dq_hbm, dq3),
+        (fresh_hbm, fresh3),
         (ct_hbm, ct_ref),
         (q_hbm, q_ref),
         (own_hbm, block_rows(g_ref, me)),
@@ -384,6 +405,23 @@
     def own_half(half):
         return own_hbm.at[half * HALF : (half + 1) * HALF]
 
+    def push_quarter(src, block, quarter, which, step, device):
+        copy = pltpu.make_async_remote_copy(
+            src_ref=src,
+            dst_ref=quarter_rows(g_ref, block, quarter),
+            send_sem=far_send.at[which, step],
+            recv_sem=far_recv.at[which, step],
+            device_id=device,
+            device_id_type=MESH,
+        )
+        copy.start()
+        sent.append(copy)
+
+    own_quarter = own_hbm.at[pl.ds(pl.multiple_of(at.y * QUARTER, 16), QUARTER)]
+    for which, device in enumerate((at.at(2, 0), at.at(2, aside), at.at(-1, aside))):
+        push_quarter(own_quarter, me, at.y, which, 0, device)
+    for half in range(2):
+        push(own_half(half), me, half, 0, at.at(0, 2 * half - 1))
     own_to_core = pltpu.make_async_remote_copy(
         src_ref=own_hbm,
         dst_ref=block_rows(g_ref, me),
@@ -394,20 +432,28 @@
     )
     own_to_core.start()
     sent.append(own_to_core)
-    for dz, station in ((1, 1), (0, 0), (-1, 3)):
-        for half in range(2):
-            if dz:
-                push(own_half(half), me, half, station, at.at(dz, 0))
-            push(own_half(half), me, half, station + (1 if dz else 0), at.at(dz, 2 * half - 1))
 
     def landed(station, half):
         block = 2 * at.station_pair(station) + at.core
         pltpu.make_async_copy(own_half(half), half_rows(g_ref, block, half), link_recv.at[station, half]).wait()
 
-    def relay(station):
-        half = 0 if station < 3 else 1
-        block = 2 * at.station_pair(station) + at.core
-        push(half_rows(g_ref, block, half), block, half, 5 + (station + 1) % 2, at.at(1 if station < 3 else -1, 0))
+    def share_x(half):
+        landed(1, half)
+        block = 2 * at.station_pair(1) + at.core
+        push(half_rows(g_ref, block, half), block, half, 2, at.at(0, 2 * half - 1))
+
+    def landed_quarter(which, step):
+        block = 2 * at.station_pair(FAR[which]) + at.core
+        quarter = (at.y - step + 4) % 4
+        source = own_hbm.at[0:QUARTER]
+        pltpu.make_async_copy(source, quarter_rows(g_ref, block, quarter), far_recv.at[which, step]).wait()
+
+    def share_far(which):
+        landed_quarter(which, 0)
+        block = 2 * at.station_pair(FAR[which]) + at.core
+        mine = quarter_rows(g_ref, block, at.y)
+        for step in (1, 3, 2):
+            push_quarter(mine, block, at.y, which, step, at.at(0, 0, step))
 
     def to_core(station):
         block = 2 * at.station_pair(station) + at.core
@@ -431,10 +477,17 @@
     loads[0].wait()
     loads[1].wait()
     prepare_weights(wk_ref, wv_ref, wkt, wvt)
+    for half in range(2):
+        push(own_half(half), me, half, 1, at.at(1, 0))
+        push(own_half(half), me, half, 3, at.at(-1, 0))
     loads[2].wait()
     loads[3].wait()
+    pack_rows(dq3, dq32, dq_ref)
+    pack_rows(fresh3, fresh32, fresh_ref)
     decode_queries(dq_ref, wkt, qh, qr)
     slot_queries(table, qr, qs2)
+    for which in range(3):
+        share_far(which)
     loads[4].wait()
     w_loads = []
     first = 0
@@ -444,16 +497,14 @@
         w_loads[-1].start()
         first += width
     decode_resident(qr, ct_ref, fresh_ref, rlen_ref, sr, ar, lo)
+    share_x(0)
+    share_x(1)
     loads[5].wait()
     prepare_queries(me, q_ref, starts, ends, qs)
 
-    for station in (1, 3):
-        for half in range(2):
-            landed(station, half)
-        relay(station)
     for half in range(2):
         landed(0, half)
-    for station in (0, 1, 3):
+    for station in (0, 1):
         to_core(station)
 
     step = functools.partial(
@@ -475,10 +526,9 @@
     from_core(N_STATION, own)
     step(own, True)
 
-    for station in (2, 4):
+    for station in (2, 3):
         for half in range(2):
             landed(station, half)
-        relay(station)
         to_core(station)
 
     def project():
@@ -516,15 +566,15 @@
         def _():
             step(pair, False)
 
-    @pl.loop(0, 5)
+    @pl.loop(0, 3)
     def _(station):
         near(station)
 
-    for station in (5, 6):
-        for half in range(2):
-            landed(station, half)
-        to_core(station)
-    for station in (5, 6):
+    for which in range(3):
+        for step_y in range(1, 4):
+            landed_quarter(which, step_y)
+        to_core(FAR[which])
+    for station in (3, 4, 5, 6):
         from_core(station, at.station_pair(station))
 
     for b in range(N_CTX):
@@ -533,7 +583,7 @@
     head_values(lo2, wv_ref, x_ref)
     sums = project()
 
-    @pl.loop(5, N_STATION)
+    @pl.loop(4, N_STATION)
     def _(station):
         pair = at.station_pair(station)
 
@@ -588,8 +638,12 @@
             pltpu.VMEM(wk.shape, BF16),
             pltpu.VMEM(wv.shape, BF16),
             pltpu.VMEM(ct.shape, BF16),
+            pltpu.VMEM((ROWS * STEPS, dq.shape[2]), BF16),
+            pltpu.VMEM((ROWS * STEPS, WIDTH), BF16),
             pltpu.VMEM(dq.shape, BF16),
             pltpu.VMEM(fresh.shape, BF16),
+            pltpu.VMEM((ROWS * STEPS, dq.shape[2]), F32),
+            pltpu.VMEM((ROWS * STEPS, WIDTH), F32),
             pltpu.VMEM(w.shape, BF16),
             pltpu.VMEM((BLOCK, HEADS * NOPE), BF16),
             pltpu.VMEM((ROWS * STEPS, HEADS * NOPE), BF16),
@@ -612,8 +666,10 @@
             pltpu.VMEM((N_TP, 16, width // 4), BF16),
             dma((8,)),
             dma((len(CHUNKS),)),
-            dma((N_STATION, 2)),
-            dma((N_STATION, 2)),
+            dma((4, 2)),
+            dma((4, 2)),
+            dma((3, 4)),
+            dma((3, 4)),
             dma((N_STATION + 1,)),
             dma((N_STATION + 1,)),
             dma((len(CHUNKS), N_TP)),
@@ -647,8 +703,8 @@
         key_weight,
         value_weight,
         cache_t,
-        decode_query.reshape(ROWS * STEPS, -1),
-        decode_latent.reshape(ROWS * STEPS, -1),
+        decode_query,
+        decode_latent,
         out_weight,
     )
 

time: 55.7 us -> 51.3 us (0.921)
  local copies, waits for them, and re-layouts: 6.36 us -> 3.35 us
  Pallas kernels: 48 us -> 46.6 us
    reshape x2 -> x0, local copies, waits for them, and re-layouts: 3.01 us -> none  [the longest x1 1.57 us: on_device(): decode_query.reshape(ROWS * STEPS, -1)]
    pallas_call x1, Pallas kernels: 48 us -> 46.6 us  [mega(): pl.pallas_call(mega_kernel, out_shape=(jax.ShapeDtypeStruct((BLOCK, HEADS...]
where the time goes in v3:
time: 51.3 us; the launch traced here: 50.6 us
  Pallas kernels  46.6 us (91%)
  local copies, waits for them, and re-layouts  3.35 us (7%)
  between operations  0.64 us (1%)
    pallas_call x1, Pallas kernels, mega(): pl.pallas_call(mega_kernel, out_shape=(jax.ShapeDtypeStruct((BLOCK, HEADS...  46.6 us
    unnamed x2, local copies, waits for them, and re-layouts  3.35 us

profile of v3, /device:TPU:97, one launch (start us, length us, event | category | flops | bytes accessed | tf_op | source)
XLA Modules:
  0.0 50.6 jit_solution(15380710753783866828)
XLA Ops:
  0.6 46.6 %latent_attention.1 = (bf16[256,1024]{1,0:T(8,128)(2,1)}, bf16[2,2,7168]{2,1,0:T(2,128)(2,1)}) custom-call(s32[8]{0:T(128)} %lens_ref.1, s32[8]{0:T(128)} %place_ref.1, s32[16]{0:T(128)} %rlen_ref.1, bf16[256,1536]{1,0:T(8,128)(2,1)} %q_hbm.1, bf16[576,256]{1,0:T(8,128)(2,1)} %bitcast.5, bf16[512,1024]{1,0:T(8,128)(2,1)} %wk_hbm.1, ...), custom_call_target="tpu_custom_call" | custom-call | tf_op jit(solution)/shard_map/latent_attention/pallas_call | solution.py:627
  47.3 1.9 %copy.15 = bf16[256,1024]{1,0:T(8,128)(2,1)} copy(bf16[256,1024]{1,0:T(8,128)(2,1)} %get-tuple-element.4) | data formatting | bytes 1048576
  49.1 1.5 %copy.16 = bf16[2,2,7168]{2,1,0:T(2,128)(2,1)} copy(bf16[2,2,7168]{2,1,0:T(2,128)(2,1)} %get-tuple-element.5) | data formatting | bytes 114688

commit v4 on v3

--- a/solution.py
+++ b/solution.py
@@ -142,19 +142,22 @@
     flat_ref[...] = wide_ref[...].astype(BF16)
 
 
-def decode_queries(dq_ref, wkt, qh, qr):
-    rows = ROWS * STEPS
+def absorb_head(window, h, wkt, qh, rows):
     eye = hot_matrix(iota((ROPE, 128), 0) == iota((ROPE, 128), 1))
     side = jnp.zeros((ROPE, 128), BF16)
     below = jnp.zeros((ROPE, LATENT), BF16)
+    weight = wkt[h * NOPE : (h + 1) * NOPE, :]
+    lat = [below, weight, below] if h % 2 else [weight, below, below]
+    rot = [side, side, side, eye] if h % 2 else [side, side, eye, side]
+    qh[h * rows : (h + 1) * rows, :LATENT] = mm(window, jnp.concatenate(lat, axis=0)).astype(BF16)
+    qh[h * rows : (h + 1) * rows, LATENT:] = mm(window, jnp.concatenate(rot, axis=0)).astype(BF16)
+
+
+def decode_queries(dq_ref, wkt, qh, qr):
+    rows = ROWS * STEPS
     for h in range(HEADS):
         base = (h // 2) * 384 + (h % 2) * 128
-        window = dq_ref[:, base : base + 256]
-        weight = wkt[h * NOPE : (h + 1) * NOPE, :]
-        lat = [below, weight, below] if h % 2 else [weight, below, below]
-        rot = [side, side, side, eye] if h % 2 else [side, side, eye, side]
-        qh[h * rows : (h + 1) * rows, :LATENT] = mm(window, jnp.concatenate(lat, axis=0)).astype(BF16)
-        qh[h * rows : (h + 1) * rows, LATENT:] = mm(window, jnp.concatenate(rot, axis=0)).astype(BF16)
+        absorb_head(dq_ref[:, base : base + 256], h, wkt, qh, rows)
     count = rows * HEADS
     order = hot_matrix(to_row_major(iota((count, count), 0)) == iota((count, count), 1))
     qr[...] = mm(order, qh[...]).astype(BF16)
@@ -206,53 +209,81 @@
     return row, first, length
 
 
-def slot_queries(table, qr, qs2):
-    per = STEPS * HEADS
-    shape = (2 * per, ROWS * per)
+def slot_picks(table, dq_ref, picks):
+    shape = (8, ROWS * STEPS)
     place = iota(shape, 0)
-    row = spread(place // per, table[0], -1)
-    pick = hot_matrix((row >= 0) & (iota(shape, 1) == row * per + place % per))
-    qs2[...] = mm(pick, qr[...]).astype(BF16)
-
-
-def slot_scores(block, g_ref, qs2, ss):
-    ss[block] = scores_of(qs2[...], latent_rows(g_ref, block, 0, LATENT), latent_rows(g_ref, block, LATENT, ROPE))
-
-
-def decode_slots(table, g_ref, qs2, ss, fresh_ref, lo_ref, out_rows):
-    per = STEPS * HEADS
-    row, first, length = table
-    lines = 2 * per
-    slot = iota((lines, BLOCK), 0) // per
-    low = spread(slot, first, 0)
-    high = low + spread(slot, length, 0)
-    fs = mm_nt(qs2[:, :LATENT], fresh_ref[:, :LATENT]) + mm_nt(qs2[:, LATENT:WIDTH], fresh_ref[:, LATENT:])
+    row = spread(place // STEPS, table[0], -1)
+    pick = hot_matrix((row >= 0) & (iota(shape, 1) == row * STEPS + place % STEPS))
+    got = mm(pick, dq_ref[...])
+    picks[...] = jnp.concatenate([got[:4, p * 384 : (p + 1) * 384] for p in range(HEADS // 2)], axis=0).astype(BF16)
+
+
+def all_slot_queries(raw, wkt, qh2, qa):
+    lines = N_CTX * 4
+    shape = (lines, N_CTX * 16)
+    place = iota(shape, 0)
+    for pair in range(HEADS // 2):
+        pick = hot_matrix(iota(shape, 1) == (place // 4) * 16 + pair * 4 + place % 4)
+        got = mm(pick, raw[...]).astype(BF16)
+        for odd in range(2):
+            absorb_head(got[:, odd * 128 : odd * 128 + 256], 2 * pair + odd, wkt, qh2, lines)
+    count = lines * HEADS
+    place = iota((count, count), 0)
+    order = (place % 32) // 4 * lines + (place // 32) * 4 + place % 4
+    qa[...] = mm(hot_matrix(order == iota((count, count), 1)), qh2[...]).astype(BF16)
+
+
+def slot_partials(me, g_ref, starts, ends, place_ref, qa, part, stat):
+    count = N_CTX * 32
+    place = iota((count, 1), 0)
+    slot = (place // 32) * 2 + (place % 4) // 2
+    low = jnp.full((count, 1), 1 << 30, jnp.int32)
+    high = jnp.full((count, 1), -1, jnp.int32)
+    for j in range(NREQ):
+        group = place_ref[j] // ROWS
+        rank = jnp.int32(0)
+        for i in range(j):
+            rank = rank + (place_ref[i] // ROWS == group).astype(jnp.int32)
+        hit = slot == group * 2 + rank
+        low = jnp.where(hit, starts[j], low)
+        high = jnp.where(hit, ends[j], high)
+    lat = latent_rows(g_ref, me, 0, LATENT)
+    s = mm(qa[:, :LATENT], lat) + mm(qa[:, LATENT:WIDTH], latent_rows(g_ref, me, LATENT, ROPE))
+    pos = me * BLOCK + iota((count, BLOCK), 1)
+    s = jnp.where((pos >= low) & (pos < high), s * FACTOR, -BIG)
+    best = jnp.max(s, axis=1, keepdims=True)
+    w = jnp.exp2(s - best)
+    weight = jnp.sum(w, axis=1, keepdims=True)
+    part[...] = (mm_nt(w.astype(BF16), lat) / weight).astype(BF16)
+    stat[...] = jnp.where(iota((count, 128), 1) < 64, best, weight)
+
+
+def merge_slots(me, table, qa, parts, stats, fresh_ref, lo_ref, out_rows):
+    row = table[0]
+    q = qa[pl.ds(pl.multiple_of(me * 32, 32), 32), :]
+    fs = mm_nt(q[:, :LATENT], fresh_ref[:, :LATENT]) + mm_nt(q[:, LATENT:WIDTH], fresh_ref[:, LATENT:])
     place, col = iota(fs.shape, 0), iota(fs.shape, 1)
-    open_ = (spread(place // per, row, -1) == col // STEPS) & (col % STEPS <= (place // HEADS) % STEPS)
+    open_ = (spread((place % 4) // 2, row, -1) == col // STEPS) & (col % STEPS <= place % STEPS)
     fs = jnp.where(open_, fs, -BIG) * FACTOR
     best = jnp.max(fs, axis=1, keepdims=True)
-    peak = jnp.full((lines, BLOCK), -BIG, F32)
-    for b in range(N_CTX):
-        pos = b * BLOCK + iota((lines, BLOCK), 1)
-        s = jnp.where((pos >= low) & (pos < high), ss[b] * FACTOR, -BIG)
-        ss[b] = s
-        peak = jnp.maximum(peak, s)
-    best = jnp.maximum(best, jnp.max(peak, axis=1, keepdims=True))
+    tops = [stats[i, :, 0:1] for i in range(N_CTX)]
+    for top in tops:
+        best = jnp.maximum(best, top)
     fw = jnp.exp2(fs - best)
-    mass = jnp.zeros((lines, BLOCK), F32)
+    weight = jnp.sum(fw, axis=1, keepdims=True)
     total = mm(fw.astype(BF16), fresh_ref[:, :LATENT])
-    for b in range(N_CTX):
-        w = jnp.exp2(ss[b] - best)
-        mass = mass + w
-        total = total + mm_nt(w.astype(BF16), latent_rows(g_ref, b, 0, LATENT))
-    weight = jnp.sum(mass, axis=1, keepdims=True) + jnp.sum(fw, axis=1, keepdims=True)
+    for i in range(N_CTX):
+        share = jnp.exp2(tops[i] - best) * stats[i, :, 64:65]
+        weight = weight + share
+        total = total + share * parts[i].astype(F32)
     slot_out = (total / weight).astype(BF16)
-    shape = (ROWS * per, lines)
-    back = iota(shape, 1)
-    back_row = spread(back // per, row, -1)
-    route = hot_matrix((back_row >= 0) & (iota(shape, 0) == back_row * per + back % per))
-    spot = iota((ROWS * per, LATENT), 0) // per
-    replaced = (spot == row[0]) | (spot == row[1])
+    per = STEPS * HEADS
+    shape = (ROWS * per, 32)
+    spot, back = iota(shape, 0), iota(shape, 1)
+    there = spread((back % 4) // 2, row, -1) == spot // per
+    route = hot_matrix(there & ((spot // HEADS) % STEPS == back % STEPS) & (spot % HEADS == back // 4))
+    line = iota((ROWS * per, LATENT), 0) // per
+    replaced = (line == row[0]) | (line == row[1])
     out_rows[...] = jnp.where(replaced, mm(route, slot_out), lo_ref[...].astype(F32)).astype(BF16)
 
 
@@ -347,9 +378,15 @@
     sr,
     ar,
     lo,
-    qs2,
-    ss,
     lo2,
+    picks,
+    raw,
+    qh2,
+    qa,
+    part,
+    stat,
+    parts,
+    stats,
     send,
     recv,
     load_sem,
@@ -362,6 +399,8 @@
     core_recv,
     sum_send,
     sum_recv,
+    slot_send,
+    slot_recv,
 ):
     at = Place()
     me, tp = at.ctx, at.tp
@@ -371,6 +410,7 @@
     peers += [at.at(1, 0), at.at(-1, 0), at.at(2, 0), at.at(0, -1), at.at(0, 1)]
     peers += [at.at(2, 1), at.at(2, -1), at.at(1, 1), at.at(1, -1), at.at(-1, 1), at.at(-1, -1)]
     peers += [(me, (tp + d) % N_TP) for d in range(1, N_TP)]
+    peers += [((me + d) % N_CTX, tp) for d in range(1, N_CTX)]
     for peer in peers:
         pl.semaphore_signal(barrier, inc=1, device_id=peer, device_id_type=MESH)
 
@@ -422,6 +462,7 @@
         push_quarter(own_quarter, me, at.y, which, 0, device)
     for half in range(2):
         push(own_half(half), me, half, 0, at.at(0, 2 * half - 1))
+        push(own_half(half), me, half, 1, at.at(1, 0))
     own_to_core = pltpu.make_async_remote_copy(
         src_ref=own_hbm,
         dst_ref=block_rows(g_ref, me),
@@ -472,41 +513,36 @@
         block = 2 * pair + 1 - at.core
         pltpu.make_async_copy(own_hbm, block_rows(g_ref, block), core_recv.at[station]).wait()
 
+    def spread_to(src, dst, kind, d):
+        copy = pltpu.make_async_remote_copy(
+            src_ref=src,
+            dst_ref=dst,
+            send_sem=slot_send.at[kind, d],
+            recv_sem=slot_recv.at[kind, d],
+            device_id=((me + d) % N_CTX, tp),
+            device_id_type=MESH,
+        )
+        copy.start()
+        slot_copies[kind].append(copy)
+
+    slot_copies = ([], [], [])
+
     starts, ends = request_table(lens_ref)
     table = slot_table(me, lens_ref, place_ref, starts)
+    loads[2].wait()
+    pack_rows(dq3, dq32, dq_ref)
+    slot_picks(table, dq_ref, picks)
+    raw[pl.ds(pl.multiple_of(me * 16, 16), 16), :] = picks[...]
+    for d in range(1, N_CTX):
+        spread_to(picks, raw.at[pl.ds(pl.multiple_of(me * 16, 16), 16)], 0, d)
     loads[0].wait()
     loads[1].wait()
     prepare_weights(wk_ref, wv_ref, wkt, wvt)
-    for half in range(2):
-        push(own_half(half), me, half, 1, at.at(1, 0))
-        push(own_half(half), me, half, 3, at.at(-1, 0))
-    loads[2].wait()
     loads[3].wait()
-    pack_rows(dq3, dq32, dq_ref)
     pack_rows(fresh3, fresh32, fresh_ref)
     decode_queries(dq_ref, wkt, qh, qr)
-    slot_queries(table, qr, qs2)
-    for which in range(3):
-        share_far(which)
-    loads[4].wait()
-    w_loads = []
-    first = 0
-    for c, width in enumerate(CHUNKS):
-        cols = slice(first, first + width)
-        w_loads.append(pltpu.make_async_copy(w_hbm.at[:, cols], w_ref.at[:, cols], w_sem.at[c]))
-        w_loads[-1].start()
-        first += width
-    decode_resident(qr, ct_ref, fresh_ref, rlen_ref, sr, ar, lo)
-    share_x(0)
-    share_x(1)
     loads[5].wait()
     prepare_queries(me, q_ref, starts, ends, qs)
-
-    for half in range(2):
-        landed(0, half)
-    for station in (0, 1):
-        to_core(station)
-
     step = functools.partial(
         attend_pair,
         me=me,
@@ -525,11 +561,34 @@
     loads[6].wait()
     from_core(N_STATION, own)
     step(own, True)
-
-    for station in (2, 3):
-        for half in range(2):
-            landed(station, half)
-        to_core(station)
+    for copy in slot_copies[0]:
+        copy.wait_recv()
+    all_slot_queries(raw, wkt, qh2, qa)
+    slot_partials(me, g_ref, starts, ends, place_ref, qa, part, stat)
+    mine = pl.ds(pl.multiple_of(me * 32, 32), 32)
+    parts[me] = part[mine, :]
+    stats[me] = stat[mine, :]
+    for d in range(1, N_CTX):
+        theirs = pl.ds(pl.multiple_of(((me + d) % N_CTX) * 32, 32), 32)
+        spread_to(part.at[theirs], parts.at[me], 1, d)
+        spread_to(stat.at[theirs], stats.at[me], 2, d)
+    for which in range(3):
+        share_far(which)
+    loads[4].wait()
+    w_loads = []
+    first = 0
+    for c, width in enumerate(CHUNKS):
+        cols = slice(first, first + width)
+        w_loads.append(pltpu.make_async_copy(w_hbm.at[:, cols], w_ref.at[:, cols], w_sem.at[c]))
+        w_loads[-1].start()
+        first += width
+    decode_resident(qr, ct_ref, fresh_ref, rlen_ref, sr, ar, lo)
+    for half in range(2):
+        landed(0, half)
+    to_core(0)
+    share_x(0)
+    share_x(1)
+    to_core(1)
 
     def project():
         copies = []
@@ -566,22 +625,28 @@
         def _():
             step(pair, False)
 
-    @pl.loop(0, 3)
+    @pl.loop(0, 2)
     def _(station):
         near(station)
 
+    for half in range(2):
+        landed(2, half)
+    to_core(2)
     for which in range(3):
         for step_y in range(1, 4):
             landed_quarter(which, step_y)
         to_core(FAR[which])
-    for station in (3, 4, 5, 6):
-        from_core(station, at.station_pair(station))
-
-    for b in range(N_CTX):
-        slot_scores(b, g_ref, qs2, ss)
-    decode_slots(table, g_ref, qs2, ss, fresh_ref, lo, lo2)
+    near(2)
+
+    for kind in (1, 2):
+        for copy in slot_copies[kind]:
+            copy.wait_recv()
+    merge_slots(me, table, qa, parts, stats, fresh_ref, lo, lo2)
     head_values(lo2, wv_ref, x_ref)
     sums = project()
+
+    for station in (4, 5, 6):
+        from_core(station, at.station_pair(station))
 
     @pl.loop(4, N_STATION)
     def _(station):
@@ -611,7 +676,7 @@
         first += width
     for _, _, copy in sums:
         copy.wait_send()
-    for copy in sent:
+    for copy in sent + slot_copies[0] + slot_copies[1] + slot_copies[2]:
         copy.wait_send()
     store.wait()
 
@@ -621,7 +686,6 @@
     vmem = pl.BlockSpec(memory_space=pltpu.VMEM)
     far = pl.BlockSpec(memory_space=pl.ANY)
     lines = ROWS * STEPS * HEADS
-    two = 2 * STEPS * HEADS
     width = w.shape[1]
     dma = pltpu.SemaphoreType.DMA
     return pl.pallas_call(
@@ -659,21 +723,29 @@
             pltpu.VMEM((lines, BLOCK), F32),
             pltpu.VMEM((lines, LATENT), F32),
             pltpu.VMEM((lines, LATENT), BF16),
-            pltpu.VMEM((two, 640), BF16),
-            pltpu.VMEM((N_CTX, two, BLOCK), F32),
             pltpu.VMEM((lines, LATENT), BF16),
+            pltpu.VMEM((16, 384), BF16),
+            pltpu.VMEM((N_CTX * 16, 384), BF16),
+            pltpu.VMEM((N_CTX * 32, 640), BF16),
+            pltpu.VMEM((N_CTX * 32, 640), BF16),
+            pltpu.VMEM((N_CTX * 32, LATENT), BF16),
+            pltpu.VMEM((N_CTX * 32, 128), F32),
+            pltpu.VMEM((N_CTX, 32, LATENT), BF16),
+            pltpu.VMEM((N_CTX, 32, 128), F32),
             pltpu.VMEM((N_TP, 16, width // 4), BF16),
             pltpu.VMEM((N_TP, 16, width // 4), BF16),
             dma((8,)),
             dma((len(CHUNKS),)),
-            dma((4, 2)),
-            dma((4, 2)),
+            dma((3, 2)),
+            dma((3, 2)),
             dma((3, 4)),
             dma((3, 4)),
             dma((N_STATION + 1,)),
             dma((N_STATION + 1,)),
             dma((len(CHUNKS), N_TP)),
             dma((len(CHUNKS), N_TP)),
+            dma((3, N_CTX)),
+            dma((3, N_CTX)),
         ],
         compiler_params=pltpu.CompilerParams(collective_id=0, has_side_effects=True, vmem_limit_bytes=60 * MIB),
         name="latent_attention",

time: 51.3 us -> 59.8 us (1.17)
  Pallas kernels: 46.6 us -> 55.6 us
    pallas_call x1, Pallas kernels: 46.6 us -> 55.6 us  [mega(): pl.pallas_call(mega_kernel, out_shape=(jax.ShapeDtypeStruct((BLOCK, HEADS...]
where the time goes in v4:
time: 59.8 us; the launch traced here: 59.6 us
  Pallas kernels  55.6 us (93%)
  local copies, waits for them, and re-layouts  3.35 us (6%)
  between operations  0.64 us (1%)
    pallas_call x1, Pallas kernels, mega(): pl.pallas_call(mega_kernel, out_shape=(jax.ShapeDtypeStruct((BLOCK, HEADS...  55.6 us
    unnamed x2, local copies, waits for them, and re-layouts  3.35 us

profile of v4, /device:TPU:97, one launch (start us, length us, event | category | flops | bytes accessed | tf_op | source)
XLA Modules:
  0.0 59.6 jit_solution(14723032856717378868)
XLA Ops:
  0.6 55.6 %latent_attention.1 = (bf16[256,1024]{1,0:T(8,128)(2,1)}, bf16[2,2,7168]{2,1,0:T(2,128)(2,1)}) custom-call(s32[8]{0:T(128)} %lens_ref.1, s32[8]{0:T(128)} %place_ref.1, s32[16]{0:T(128)} %rlen_ref.1, bf16[256,1536]{1,0:T(8,128)(2,1)} %q_hbm.1, bf16[576,256]{1,0:T(8,128)(2,1)} %bitcast.5, bf16[512,1024]{1,0:T(8,128)(2,1)} %wk_hbm.1, ...), custom_call_target="tpu_custom_call" | custom-call | tf_op jit(solution)/shard_map/latent_attention/pallas_call | solution.py:691
  56.2 1.9 %copy.15 = bf16[256,1024]{1,0:T(8,128)(2,1)} copy(bf16[256,1024]{1,0:T(8,128)(2,1)} %get-tuple-element.4) | data formatting | bytes 1048576
  58.1 1.5 %copy.16 = bf16[2,2,7168]{2,1,0:T(2,128)(2,1)} copy(bf16[2,2,7168]{2,1,0:T(2,128)(2,1)} %get-tuple-element.5) | data formatting | bytes 114688

commit v5 on v3

--- a/solution.py
+++ b/solution.py
@@ -29,7 +29,7 @@
 QUARTER = WIDTH // 4
 N_Z = 4
 N_STATION = 7
-FAR = (5, 6, 4)
+FAR = (5, 6)
 CHUNKS = (2048, 2048, 2048, 1024)
 
 
@@ -369,7 +369,7 @@
     peers = [at.sibling()]
     aside = 1 - 2 * (at.y % 2)
     peers += [at.at(1, 0), at.at(-1, 0), at.at(2, 0), at.at(0, -1), at.at(0, 1)]
-    peers += [at.at(2, 1), at.at(2, -1), at.at(1, 1), at.at(1, -1), at.at(-1, 1), at.at(-1, -1)]
+    peers += [at.at(2, 1), at.at(2, -1)]
     peers += [(me, (tp + d) % N_TP) for d in range(1, N_TP)]
     for peer in peers:
         pl.semaphore_signal(barrier, inc=1, device_id=peer, device_id_type=MESH)
@@ -418,7 +418,7 @@
         sent.append(copy)
 
     own_quarter = own_hbm.at[pl.ds(pl.multiple_of(at.y * QUARTER, 16), QUARTER)]
-    for which, device in enumerate((at.at(2, 0), at.at(2, aside), at.at(-1, aside))):
+    for which, device in enumerate((at.at(2, 0), at.at(2, aside))):
         push_quarter(own_quarter, me, at.y, which, 0, device)
     for half in range(2):
         push(own_half(half), me, half, 0, at.at(0, 2 * half - 1))
@@ -438,9 +438,10 @@
         pltpu.make_async_copy(own_half(half), half_rows(g_ref, block, half), link_recv.at[station, half]).wait()
 
     def share_x(half):
-        landed(1, half)
-        block = 2 * at.station_pair(1) + at.core
-        push(half_rows(g_ref, block, half), block, half, 2, at.at(0, 2 * half - 1))
+        for station in (1, 3):
+            landed(station, half)
+            block = 2 * at.station_pair(station) + at.core
+            push(half_rows(g_ref, block, half), block, half, station + 1, at.at(0, 2 * half - 1))
 
     def landed_quarter(which, step):
         block = 2 * at.station_pair(FAR[which]) + at.core
@@ -486,27 +487,8 @@
     pack_rows(fresh3, fresh32, fresh_ref)
     decode_queries(dq_ref, wkt, qh, qr)
     slot_queries(table, qr, qs2)
-    for which in range(3):
-        share_far(which)
-    loads[4].wait()
-    w_loads = []
-    first = 0
-    for c, width in enumerate(CHUNKS):
-        cols = slice(first, first + width)
-        w_loads.append(pltpu.make_async_copy(w_hbm.at[:, cols], w_ref.at[:, cols], w_sem.at[c]))
-        w_loads[-1].start()
-        first += width
-    decode_resident(qr, ct_ref, fresh_ref, rlen_ref, sr, ar, lo)
-    share_x(0)
-    share_x(1)
     loads[5].wait()
     prepare_queries(me, q_ref, starts, ends, qs)
-
-    for half in range(2):
-        landed(0, half)
-    for station in (0, 1):
-        to_core(station)
-
     step = functools.partial(
         attend_pair,
         me=me,
@@ -525,11 +507,26 @@
     loads[6].wait()
     from_core(N_STATION, own)
     step(own, True)
-
-    for station in (2, 3):
-        for half in range(2):
-            landed(station, half)
-        to_core(station)
+    for half in range(2):
+        slot_scores(2 * own + half, g_ref, qs2, ss)
+    for which in range(2):
+        share_far(which)
+    loads[4].wait()
+    w_loads = []
+    first = 0
+    for c, width in enumerate(CHUNKS):
+        cols = slice(first, first + width)
+        w_loads.append(pltpu.make_async_copy(w_hbm.at[:, cols], w_ref.at[:, cols], w_sem.at[c]))
+        w_loads[-1].start()
+        first += width
+    decode_resident(qr, ct_ref, fresh_ref, rlen_ref, sr, ar, lo)
+    for half in range(2):
+        landed(0, half)
+    to_core(0)
+    share_x(0)
+    share_x(1)
+    to_core(1)
+    to_core(3)
 
     def project():
         copies = []
@@ -566,19 +563,28 @@
         def _():
             step(pair, False)
 
-    @pl.loop(0, 3)
+    @pl.loop(0, 2)
     def _(station):
         near(station)
 
-    for which in range(3):
+    for station in (2, 4):
+        for half in range(2):
+            landed(station, half)
+        to_core(station)
+    near(2)
+    for which in range(2):
         for step_y in range(1, 4):
             landed_quarter(which, step_y)
         to_core(FAR[which])
+    for station in range(3):
+        for half in range(2):
+            slot_scores(2 * at.station_pair(station) + half, g_ref, qs2, ss)
     for station in (3, 4, 5, 6):
         from_core(station, at.station_pair(station))
 
-    for b in range(N_CTX):
-        slot_scores(b, g_ref, qs2, ss)
+    for station in (3, 4, 5, 6):
+        for half in range(2):
+            slot_scores(2 * at.station_pair(station) + half, g_ref, qs2, ss)
     decode_slots(table, g_ref, qs2, ss, fresh_ref, lo, lo2)
     head_values(lo2, wv_ref, x_ref)
     sums = project()
@@ -666,10 +672,10 @@
             pltpu.VMEM((N_TP, 16, width // 4), BF16),
             dma((8,)),
             dma((len(CHUNKS),)),
-            dma((4, 2)),
-            dma((4, 2)),
-            dma((3, 4)),
-            dma((3, 4)),
+            dma((5, 2)),
+            dma((5, 2)),
+            dma((2, 4)),
+            dma((2, 4)),
             dma((N_STATION + 1,)),
             dma((N_STATION + 1,)),
             dma((len(CHUNKS), N_TP)),

time: 51.3 us -> 50.5 us (0.984)
  no operation moved by 1% of the time
where the time goes in v5:
time: 50.5 us; the launch traced here: 50.3 us
  Pallas kernels  46.3 us (92%)
  local copies, waits for them, and re-layouts  3.35 us (7%)
  between operations  0.64 us (1%)
    pallas_call x1, Pallas kernels, mega(): pl.pallas_call(mega_kernel, out_shape=(jax.ShapeDtypeStruct((BLOCK, HEADS...  46.3 us
    unnamed x2, local copies, waits for them, and re-layouts  3.35 us

profile of v5, /device:TPU:97, one launch (start us, length us, event | category | flops | bytes accessed | tf_op | source)
XLA Modules:
  0.0 50.3 jit_solution(10664525844061074933)
XLA Ops:
  0.6 46.3 %latent_attention.1 = (bf16[256,1024]{1,0:T(8,128)(2,1)}, bf16[2,2,7168]{2,1,0:T(2,128)(2,1)}) custom-call(s32[8]{0:T(128)} %lens_ref.1, s32[8]{0:T(128)} %place_ref.1, s32[16]{0:T(128)} %rlen_ref.1, bf16[256,1536]{1,0:T(8,128)(2,1)} %q_hbm.1, bf16[576,256]{1,0:T(8,128)(2,1)} %bitcast.5, bf16[512,1024]{1,0:T(8,128)(2,1)} %wk_hbm.1, ...), custom_call_target="tpu_custom_call" | custom-call | tf_op jit(solution)/shard_map/latent_attention/pallas_call | solution.py:633
  47.0 1.9 %copy.15 = bf16[256,1024]{1,0:T(8,128)(2,1)} copy(bf16[256,1024]{1,0:T(8,128)(2,1)} %get-tuple-element.4) | data formatting | bytes 1048576
  48.8 1.5 %copy.16 = bf16[2,2,7168]{2,1,0:T(2,128)(2,1)} copy(bf16[2,2,7168]{2,1,0:T(2,128)(2,1)} %get-tuple-element.5) | data formatting | bytes 114688

commit v6 on v5

--- a/solution.py
+++ b/solution.py
@@ -571,11 +571,11 @@
         for half in range(2):
             landed(station, half)
         to_core(station)
-    near(2)
     for which in range(2):
         for step_y in range(1, 4):
             landed_quarter(which, step_y)
         to_core(FAR[which])
+    near(2)
     for station in range(3):
         for half in range(2):
             slot_scores(2 * at.station_pair(station) + half, g_ref, qs2, ss)

time: 50.5 us -> 48.8 us (0.966)
  Pallas kernels: 46.3 us -> 44.4 us
    pallas_call x1, Pallas kernels: 46.3 us -> 44.4 us  [mega(): pl.pallas_call(mega_kernel, out_shape=(jax.ShapeDtypeStruct((BLOCK, HEADS...]
where the time goes in v6:
time: 48.8 us; the launch traced here: 48.4 us
  Pallas kernels  44.4 us (91%)
  local copies, waits for them, and re-layouts  3.35 us (7%)
  between operations  0.64 us (1%)
    pallas_call x1, Pallas kernels, mega(): pl.pallas_call(mega_kernel, out_shape=(jax.ShapeDtypeStruct((BLOCK, HEADS...  44.4 us
    unnamed x2, local copies, waits for them, and re-layouts  3.35 us

profile of v6, /device:TPU:97, one launch (start us, length us, event | category | flops | bytes accessed | tf_op | source)
XLA Modules:
  0.0 48.4 jit_solution(15571363201418150998)
XLA Ops:
  0.6 44.4 %latent_attention.1 = (bf16[256,1024]{1,0:T(8,128)(2,1)}, bf16[2,2,7168]{2,1,0:T(2,128)(2,1)}) custom-call(s32[8]{0:T(128)} %lens_ref.1, s32[8]{0:T(128)} %place_ref.1, s32[16]{0:T(128)} %rlen_ref.1, bf16[256,1536]{1,0:T(8,128)(2,1)} %q_hbm.1, bf16[576,256]{1,0:T(8,128)(2,1)} %bitcast.5, bf16[512,1024]{1,0:T(8,128)(2,1)} %wk_hbm.1, ...), custom_call_target="tpu_custom_call" | custom-call | tf_op jit(solution)/shard_map/latent_attention/pallas_call | solution.py:633
  45.0 1.9 %copy.15 = bf16[256,1024]{1,0:T(8,128)(2,1)} copy(bf16[256,1024]{1,0:T(8,128)(2,1)} %get-tuple-element.4) | data formatting | bytes 1048576
  46.9 1.5 %copy.16 = bf16[2,2,7168]{2,1,0:T(2,128)(2,1)} copy(bf16[2,2,7168]{2,1,0:T(2,128)(2,1)} %get-tuple-element.5) | data formatting | bytes 114688

commit v7 on v6

--- a/solution.py
+++ b/solution.py
@@ -421,6 +421,8 @@
     for which, device in enumerate((at.at(2, 0), at.at(2, aside))):
         push_quarter(own_quarter, me, at.y, which, 0, device)
     for half in range(2):
+        push(own_half(half), me, half, 1, at.at(1, 0))
+        push(own_half(half), me, half, 3, at.at(-1, 0))
         push(own_half(half), me, half, 0, at.at(0, 2 * half - 1))
     own_to_core = pltpu.make_async_remote_copy(
         src_ref=own_hbm,
@@ -478,9 +480,6 @@
     loads[0].wait()
     loads[1].wait()
     prepare_weights(wk_ref, wv_ref, wkt, wvt)
-    for half in range(2):
-        push(own_half(half), me, half, 1, at.at(1, 0))
-        push(own_half(half), me, half, 3, at.at(-1, 0))
     loads[2].wait()
     loads[3].wait()
     pack_rows(dq3, dq32, dq_ref)

time: 48.8 us -> 48.8 us (level)
  no operation moved by 1% of the time
where the time goes in v7:
time: 48.8 us; the launch traced here: 48.4 us
  Pallas kernels  44.4 us (91%)
  local copies, waits for them, and re-layouts  3.35 us (7%)
  between operations  0.64 us (1%)
    pallas_call x1, Pallas kernels, mega(): pl.pallas_call(mega_kernel, out_shape=(jax.ShapeDtypeStruct((BLOCK, HEADS...  44.4 us
    unnamed x2, local copies, waits for them, and re-layouts  3.35 us

profile of v7, /device:TPU:97, one launch (start us, length us, event | category | flops | bytes accessed | tf_op | source)
XLA Modules:
  0.0 48.4 jit_solution(13372320107655733218)
XLA Ops:
  0.6 44.4 %latent_attention.1 = (bf16[256,1024]{1,0:T(8,128)(2,1)}, bf16[2,2,7168]{2,1,0:T(2,128)(2,1)}) custom-call(s32[8]{0:T(128)} %lens_ref.1, s32[8]{0:T(128)} %place_ref.1, s32[16]{0:T(128)} %rlen_ref.1, bf16[256,1536]{1,0:T(8,128)(2,1)} %q_hbm.1, bf16[576,256]{1,0:T(8,128)(2,1)} %bitcast.5, bf16[512,1024]{1,0:T(8,128)(2,1)} %wk_hbm.1, ...), custom_call_target="tpu_custom_call" | custom-call | tf_op jit(solution)/shard_map/latent_attention/pallas_call | solution.py:632
  45.0 1.9 %copy.15 = bf16[256,1024]{1,0:T(8,128)(2,1)} copy(bf16[256,1024]{1,0:T(8,128)(2,1)} %get-tuple-element.4) | data formatting | bytes 1048576
  46.9 1.5 %copy.16 = bf16[2,2,7168]{2,1,0:T(2,128)(2,1)} copy(bf16[2,2,7168]{2,1,0:T(2,128)(2,1)} %get-tuple-element.5) | data formatting | bytes 114688
